TPU v7x, 512 devices: a whole 4x8x8 slice. The times are simulated.
512 devices in a mesh: dp: 8 (over z), ctx: 16 (over y, x_lo), head: 4 (over x_hi, core).
Axes of the slice: x: 4 (x_hi: 2, x_lo: 2; x = x_hi * 2 + x_lo), y: 8, z: 8, core: 2. Of those that a mesh axis runs over, the one named last changes fastest.
Arguments:
- queries: bfloat16 [8, 2048, 64, 128], P('dp', 'ctx', 'head'), may hold values from -4.5 to 4.5
- keys: bfloat16 [8, 2048, 8, 128], P('dp', 'ctx', 'head'), may hold values from -4.5 to 4.5
- values: bfloat16 [8, 2048, 8, 128], P('dp', 'ctx', 'head'), may hold values from -6 to 6
- map_query: bfloat16 [64, 128, 64], P('head'), may hold values from -1.390625 to 1.390625
- map_key: bfloat16 [64, 128, 64], P('head'), may hold values from -1.390625 to 1.390625
Outputs:
- grad_query_map: float32 [64, 128, 64], P('head')
- grad_key_map: float32 [64, 128, 64], P('head')
- head_loss: float32 [64], P('head')
All inputs are finite; a program needn't handle non-finite values.
Results may differ from a plain program's by a relative error of at most 0.0038.
Values may be sent and summed in bfloat16 or wider, within the bound.
No kernel may reach another device: no remote copies, remote signals or barrier semaphores. Data moves between devices by JAX's collectives and lax.ppermute only.
A program may use at most 128 MiB of HBM per device.

v0:
```python
import jax
import jax.numpy as jnp
from jax import lax
from jax.sharding import PartitionSpec as P

HIGH = lax.Precision.HIGHEST


def entering(shard, axis, join, neutral, backward):
    count = lax.axis_size(axis)
    place = lax.axis_index(axis)
    ahead = count - 1 - place if backward else place
    gathered = jax.tree.map(
        lambda a, kind: lax.all_gather(a.astype(kind), axis), shard, (jnp.bfloat16, jnp.bfloat16)
    )
    state = jax.tree.map(lambda a, e: jnp.zeros_like(a) + jnp.asarray(e, a.dtype), shard, neutral)

    def one(turn, state):
        source = count - 1 - turn if backward else turn
        return join(
            state,
            jax.tree.map(
                lambda a, own: lax.dynamic_index_in_dim(a, source, 0, False).astype(own.dtype),
                gathered,
                shard,
            ),
        )

    return lax.fori_loop(0, ahead, one, state)


def narrow(pattern, left_side, right_side):
    return jnp.einsum(pattern, left_side, right_side, preferred_element_type=jnp.float32)


def precise(pattern, left_side, right_side):
    return jnp.einsum(
        pattern, left_side, right_side, precision=HIGH, preferred_element_type=jnp.float32
    )


def features(inputs, mapping):
    logits = narrow("thd,hdf->thf", inputs, mapping)
    positive = jax.nn.softmax(logits, axis=-1)
    negative = jax.nn.softmax(-logits, axis=-1)
    joined = jnp.concatenate([positive, negative], -1).astype(jnp.bfloat16)
    return (joined, positive, negative)


def map_gradient(inputs, positive, negative, feature_gradient):
    half_width = positive.shape[-1]
    positive_gradient = feature_gradient[..., :half_width]
    negative_gradient = feature_gradient[..., half_width:]
    logit_gradient = positive * (
        positive_gradient - jnp.sum(positive_gradient * positive, -1, keepdims=True)
    )
    logit_gradient = logit_gradient - negative * (
        negative_gradient - jnp.sum(negative_gradient * negative, -1, keepdims=True)
    )
    return precise("thd,thf->hdf", inputs, logit_gradient)


def combine_sum(earlier, later_part):
    return jax.tree.map(jnp.add, earlier, later_part)


def absorb(carried, grouped, row_start, key_block, value_block, key_start, score_scale):
    row_count = grouped.shape[0]
    key_count = key_block.shape[0]

    def accumulate(running, scores):
        row_peak, mass_sum, accumulated = running
        new_peak = jnp.maximum(row_peak, jnp.max(scores, -1))
        factor = jnp.exp(row_peak - new_peak)
        expo = jnp.exp(scores - new_peak[..., None])
        mass_sum = mass_sum * factor + jnp.sum(expo, -1)
        accumulated = accumulated * jnp.transpose(factor, (2, 0, 1))[..., None]
        accumulated = accumulated + narrow("kgts,skd->tkgd", expo.astype(jnp.bfloat16), value_block)
        return (new_peak, mass_sum, accumulated)

    def whole_block(running):
        scores = narrow("tkgd,skd->kgts", grouped, key_block) * score_scale
        return accumulate(running, scores)

    def diagonal_block(running):
        scores = narrow("tkgd,skd->kgts", grouped, key_block) * score_scale
        query_pos = row_start + jnp.arange(row_count)
        key_pos = key_start + jnp.arange(key_count)
        allowed = key_pos[None, :] <= query_pos[:, None]
        scores = jnp.where(allowed[None, None], scores, -jnp.inf)
        return accumulate(running, scores)

    def skip_block(running):
        return running

    skipped = key_start > row_start + row_count - 1
    complete = key_start + key_count - 1 <= row_start
    branch = jnp.where(skipped, 0, jnp.where(complete, 1, 2)).astype(jnp.int32)
    return lax.switch(branch, [skip_block, whole_block, diagonal_block], carried)


def shards(queries, keys, values, map_query, map_key):
    local_queries = queries[0]
    local_keys = keys[0]
    local_values = values[0]
    block_rows, query_heads, head_size = local_queries.shape
    value_heads = local_keys.shape[1]
    group_size = query_heads // value_heads
    block_index = lax.axis_index("ctx")
    ctx_count = lax.axis_size("ctx")
    query_start = block_index * block_rows
    score_scale = head_size ** (-0.5)
    grouped_queries = local_queries.reshape(block_rows, value_heads, group_size, head_size)
    pieces = [(grouped_queries, query_start)]

    def absorb_all(carries, key_block, value_block, key_start):
        return tuple(
            (
                absorb(running, grouped, row_start, key_block, value_block, key_start, score_scale)
                for running, (grouped, row_start) in zip(carries, pieces)
            )
        )

    initial = tuple(
        (
            (
                jnp.full((value_heads, group_size, grouped.shape[0]), -1e30, jnp.float32),
                jnp.zeros((value_heads, group_size, grouped.shape[0]), jnp.float32),
                jnp.zeros((grouped.shape[0], value_heads, group_size, head_size), jnp.float32),
            )
            for grouped, row_start in pieces
        )
    )
    carried = initial
    key_piece = lax.all_gather(keys, "ctx", axis=1, tiled=True)[0]
    value_piece = lax.all_gather(values, "ctx", axis=1, tiled=True)[0]
    step_count = key_piece.shape[0] // block_rows
    key_steps = key_piece.reshape(step_count, block_rows, value_heads, head_size)
    value_steps = value_piece.reshape(step_count, block_rows, value_heads, head_size)

    def one_step(running, block_item):
        key_block, value_block, step_index = block_item
        return (absorb_all(running, key_block, value_block, step_index * block_rows), None)

    carried, unused = lax.scan(
        one_step, carried, (key_steps, value_steps, jnp.arange(step_count, dtype=jnp.int32))
    )
    outputs = []
    for row_peak, mass_sum, accumulated in carried:
        outputs.append(
            (accumulated / jnp.transpose(mass_sum, (2, 0, 1))[..., None]).reshape(
                accumulated.shape[0], query_heads, head_size
            )
        )
    target = outputs[0]
    wide_keys = jnp.broadcast_to(
        local_keys[:, :, None, :], (block_rows, value_heads, group_size, head_size)
    ).reshape(block_rows, query_heads, head_size)
    wide_values = jnp.broadcast_to(
        local_values[:, :, None, :], (block_rows, value_heads, group_size, head_size)
    ).reshape(block_rows, query_heads, head_size)
    query_features, query_positive, query_negative = features(local_queries, map_query)
    key_features, key_positive, key_negative = features(wide_keys, map_key)
    block_state = narrow("shf,shd->hfd", key_features, wide_values)
    block_total = jnp.sum(key_features, 0, dtype=jnp.float32)
    state_sum, total_sum = entering(
        (block_state, block_total),
        "ctx",
        combine_sum,
        (jnp.zeros_like(block_state), jnp.zeros_like(block_total)),
        False,
    )
    positions = jnp.arange(block_rows)
    causal = positions[:, None] >= positions[None, :]
    scores = jnp.where(causal[None], narrow("thf,shf->hts", query_features, key_features), 0.0)
    numerator = precise("hts,shd->thd", scores, wide_values) + precise(
        "thf,hfd->thd", query_features, state_sum
    )
    denominator = jnp.transpose(jnp.sum(scores, -1)) + precise(
        "thf,hf->th", query_features, total_sum
    )
    student = numerator / denominator[..., None]
    token_count = lax.axis_size("dp") * ctx_count * block_rows
    residual = student - target
    loss_part = jnp.sum(residual * residual, (0, 2)) / token_count
    student_gradient = 2.0 * residual / token_count
    gradient_numerator = student_gradient / denominator[..., None]
    gradient_denominator = -jnp.sum(student_gradient * student, -1) / denominator
    block_later = precise("thf,thd->hfd", query_features, gradient_numerator)
    block_later_total = precise("thf,th->hf", query_features, gradient_denominator)
    suffix_state, suffix_totals = entering(
        (block_later, block_later_total),
        "ctx",
        combine_sum,
        (jnp.zeros_like(block_later), jnp.zeros_like(block_later_total)),
        True,
    )
    weights = (
        precise("thd,shd->hts", gradient_numerator, wide_values)
        + jnp.transpose(gradient_denominator)[:, :, None]
    )
    weights = jnp.where(causal[None], weights, 0.0)
    query_gradient = (
        precise("hts,shf->thf", weights, key_features)
        + precise("hfd,thd->thf", state_sum, gradient_numerator)
        + gradient_denominator[:, :, None] * total_sum[None]
    )
    key_gradient = (
        precise("hts,thf->shf", weights, query_features)
        + precise("hfd,shd->shf", suffix_state, wide_values)
        + suffix_totals[None]
    )
    query_map_gradient = map_gradient(local_queries, query_positive, query_negative, query_gradient)
    key_map_gradient = map_gradient(wide_keys, key_positive, key_negative, key_gradient)
    grad_query_map, grad_key_map, head_loss = lax.psum(
        (query_map_gradient, key_map_gradient, loss_part), ("dp", "ctx")
    )
    return (grad_query_map, grad_key_map, head_loss)


def solution(mesh):
    placed = (
        P("dp", "ctx", "head", None),
        P("dp", "ctx", "head", None),
        P("dp", "ctx", "head", None),
        P("head", None, None),
        P("head", None, None),
    )
    return jax.shard_map(
        shards,
        mesh=mesh,
        in_specs=placed,
        out_specs=(P("head", None, None), P("head", None, None), P("head")),
        check_vma=False,
    )
```

profile of v0, /device:TPU:4, one launch (start us, length us, event | category | flops | bytes accessed | tf_op | source)
XLA Modules:
  0.0 1786.7 jit_solution(8034703201000215556)
XLA Ops:
  7.2 1.5 copy.68
  8.8 1.5 copy.69
  12.1 1.6 fusion.72
  13.6 2.5 fusion.73
  16.3 1.6 fusion.70
  17.9 1.6 fusion.71
  19.7 1.3 fusion.61
  23.7 34.0 %all-gather.1 = bf16[256,128]{1,0:T(8,128)(2,1)S(1)} all-gather(bf16[16,128]{1,0:T(8,128)(2,1)S(1)} %fusion.60), channel_id=3, replica_groups=mesh['dp'=8,'ctx'=16,'head'=4] {'ctx'}, dimensions={0}, use_global_device_ids=true | all-gather | bytes 69632 | tf_op jit(solution)/shard_map/all_gather | solution.py:14
  58.1 1.8 convolution_bitcast_fusion.5
  60.0 25.9 %all-gather.9.cloned.1.call-done = bf16[1,2048,2,128]{3,1,2,0:T(8,128)(2,1)} async-done(((bf16[1,128,2,128]{3,1,2,0:T(8,128)(2,1)}), bf16[1,2048,2,128]{3,1,2,0:T(8,128)(2,1)}) %all-gather.9.cloned.1.call-update) | async-done | bytes 1048592 | tf_op jit(solution)/shard_map/all_gather | solution.py:135
  85.9 74.1 %all-gather.11.cloned.1.call-done = bf16[1,2048,2,128]{3,1,2,0:T(8,128)(2,1)} async-done(((bf16[1,128,2,128]{3,1,2,0:T(8,128)(2,1)}), bf16[1,2048,2,128]{3,1,2,0:T(8,128)(2,1)}) %all-gather.11.cloned.1.call-update) | async-done | bytes 1048592 | tf_op jit(solution)/shard_map/all_gather | solution.py:136
  160.1 36.9 %while.46 = (s32[]{:T(128)}, f32[2,8,128]{2,1,0:T(8,128)S(1)}, f32[2,8,128]{2,1,0:T(8,128)S(1)}, f32[128,2,8,128]{3,0,2,1:T(8,128)S(1)}, s32[16]{0:T(128)S(1)}, ...) while((s32[]{:T(128)}, f32[2,8,128]{2,1,0:T(8,128)S(1)}, ...), condition=%wide.region_20.21_spmd, body=%wide.region_12.20_spmd.sunk | while | flops 136599808 | bytes 6326697 | solution.py:145
  162.3 1.3 conditional.2
  197.0 1.3 broadcast_divide_fusion
  198.3 2.5 copy.73
  200.9 147.7 %all-gather.13.cloned.1.call-done = bf16[256,128,128]{2,1,0:T(8,128)(2,1)} async-done(((bf16[16,128,128]{2,1,0:T(8,128)(2,1)}), bf16[256,128,128]{2,1,0:T(8,128)(2,1)}) %all-gather.13.cloned.1.call-update) | async-done | bytes 8388624 | tf_op jit(solution)/shard_map/all_gather | solution.py:14
  349.2 3.0 multiply_reduce_fusion
  352.2 2.0 convolution_convert_fusion.1
  354.4 2.1 fusion.65
  356.5 56.7 %all-gather.3 = bf16[256,128]{1,0:T(8,128)(2,1)S(1)} all-gather(bf16[16,128]{1,0:T(8,128)(2,1)S(1)} %convert_element_type.51), channel_id=5, replica_groups=mesh['dp'=8,'ctx'=16,'head'=4] {'ctx'}, dimensions={0}, use_global_device_ids=true | all-gather | bytes 69632 | tf_op jit(solution)/shard_map/all_gather | solution.py:14
  416.2 2.3 fusion.66
  418.5 1.5 convolution_bitcast_fusion.9
  420.0 138.1 %all-gather.15.cloned.1.call-done = bf16[256,128,128]{2,1,0:T(8,128)(2,1)} async-done(((bf16[16,128,128]{2,1,0:T(8,128)(2,1)}), bf16[256,128,128]{2,1,0:T(8,128)(2,1)}) %all-gather.15.cloned.1.call-update) | async-done | bytes 8388624 | tf_op jit(solution)/shard_map/all_gather | solution.py:14
  558.2 20.0 %while.47 = (s32[]{:T(128)}, f32[16,128,128]{2,1,0:T(8,128)S(1)}, f32[16,128]{1,0:T(8,128)S(1)}, s32[]{:T(128)}, bf16[16,16,128,128]{3,2,1,0:T(8,128)(2,1)}, /*i...) while((s32[]{:T(128)}, f32[16,128,128]{2,1,0:T(8,128)S(1)}, ...), condition=%wide.region_26.27_spmd, body=%wide.region_25.26_spmd.sunk | while | flops 528390 | bytes 2642083 | solution.py:29
  558.3 1.4 convert_add_fusion.10
  562.3 1.3 convert_add_fusion.10
  578.2 2.5 fusion.24
  581.0 1.4 convolution_bitcast_fusion.8
  582.5 304.0 %psum.23 = f32[16]{0:T(128)} all-reduce(f32[16]{0:T(128)S(1)} %broadcast_multiply_fusion), channel_id=1, replica_groups=mesh['dp'=8,'ctx'=16,'head'=4] {'dp','ctx'}, use_global_device_ids=true, to_apply=%region_31.32 | all-reduce | flops 16 | bytes 128 | tf_op jit(solution)/shard_map/psum | solution.py:215
  886.5 889.9 %all-reduce.3.cloned.1.call-done = (f32[16,128,64]{1,2,0:T(8,128)}, f32[16,128,64]{1,2,0:T(8,128)}) async-done(((f32[16,128,64]{1,2,0:T(8,128)}, f32[16,128,64]{1,2,0:T(8,128)}), (f32[16,128,64]{1,2,0:T(8,128)}, f32[16,128,64]{1,2,0:T(8,128)})) %all-reduce.3.cloned.1.call-update) | async-done | bytes 1048592 | tf_op jit(solution)/shard_map/psum | solution.py:215
  1776.4 1.9 copy.168
  1778.3 1.9 copy.169
  (157 shorter events, 52.3 us)
Async XLA Ops:
  7.2 4.9 copy-start
  7.2 78.7 %all-gather.9.cloned.1.call-start = ((), (), s32[]{:S(2)}) async-start(), calls=%async_computation | async-start | bytes 1114112 | tf_op jit(solution)/shard_map/all_gather | solution.py:135
  8.7 151.2 %all-gather.11.cloned.1.call-start = ((), (), s32[]{:S(2)}) async-start(), calls=%async_computation.1 | async-start | bytes 1114112 | tf_op jit(solution)/shard_map/all_gather | solution.py:136
  10.3 338.2 %all-gather.13.cloned.1.call-start = ((), (), s32[]{:S(2)}) async-start(), calls=%async_computation.2 | async-start | bytes 8912896 | tf_op jit(solution)/shard_map/all_gather | solution.py:14
  13.6 7.4 copy-start.13
  16.3 143.7 %copy-start.1 = (bf16[128,2,8,128]{3,0,2,1:T(8,128)(2,1)}, bf16[128,2,8,128]{3,0,2,1:T(8,128)(2,1)S(1)}, u32[]{:S(2)}) copy-start(bf16[128,2,8,128]{3,0,2,1:T(8,128)(2,1)S(1)} %broadcast_in_dim.52) | copy-start | bytes 1572868
  17.9 142.0 %copy-start.3 = (f32[128,16,64]{0,2,1:T(8,128)}, f32[128,16,64]{0,2,1:T(8,128)S(1)}, u32[]{:S(2)}) copy-start(f32[128,16,64]{0,2,1:T(8,128)S(1)} %get-tuple-element.537) | copy-start | bytes 1572868
  19.6 2.7 copy-start.5
  19.7 329.0 %copy-start.7 = (bf16[128,16,64]{0,2,1:T(8,128)(2,1)}, bf16[128,16,64]{0,2,1:T(8,128)(2,1)S(1)}, u32[]{:S(2)}) copy-start(bf16[128,16,64]{0,2,1:T(8,128)(2,1)S(1)} %get-tuple-element.549) | copy-start | bytes 786436
  21.0 327.7 %copy-start.10 = (bf16[128,16,64]{0,2,1:T(8,128)(2,1)}, bf16[128,16,64]{0,2,1:T(8,128)(2,1)S(1)}, u32[]{:S(2)}) copy-start(bf16[128,16,64]{0,2,1:T(8,128)(2,1)S(1)} %get-tuple-element.546) | copy-start | bytes 786436
  22.3 535.8 %all-gather.15.cloned.1.call-start = ((), (), s32[]{:S(2)}) async-start(), calls=%async_computation.3 | async-start | bytes 8912896 | tf_op jit(solution)/shard_map/all_gather | solution.py:14
  349.2 3.0 copy-start.8
  349.2 3.0 copy-start.11
  354.3 1422.2 %all-reduce.3.cloned.1.call-start = ((), (), s32[]{:S(2)}) async-start(), calls=%async_computation.4 | async-start | bytes 2097152 | tf_op jit(solution)/shard_map/psum | solution.py:215
  354.3 61.5 %copy-start.14 = (f32[128,16,64]{0,2,1:T(8,128)S(1)}, f32[128,16,64]{0,2,1:T(8,128)}, u32[]{:S(2)}) copy-start(f32[128,16,64]{0,2,1:T(8,128)} %copy-done.13) | copy-start | bytes 1572868
  354.3 61.5 %copy-start.15 = (f32[128,16,64]{0,2,1:T(8,128)S(1)}, f32[128,16,64]{0,2,1:T(8,128)}, u32[]{:S(2)}) copy-start(f32[128,16,64]{0,2,1:T(8,128)} %get-tuple-element.543) | copy-start | bytes 1572868
  354.4 61.8 %copy-start.9 = (bf16[128,16,64]{0,2,1:T(8,128)(2,1)S(1)}, bf16[128,16,64]{0,2,1:T(8,128)(2,1)}, u32[]{:S(2)}) copy-start(bf16[128,16,64]{0,2,1:T(8,128)(2,1)} %copy-done.7) | copy-start | bytes 786436
  354.4 61.8 %copy-start.12 = (bf16[128,16,64]{0,2,1:T(8,128)(2,1)S(1)}, bf16[128,16,64]{0,2,1:T(8,128)(2,1)}, u32[]{:S(2)}) copy-start(bf16[128,16,64]{0,2,1:T(8,128)(2,1)} %copy-done.10) | copy-start | bytes 786436
  354.4 64.1 %copy-start.16 = (bf16[1,128,16,128]{3,2,1,0:T(8,128)(2,1)S(1)}, bf16[1,128,16,128]{3,2,1,0:T(8,128)(2,1)}, u32[]{:S(2)}) copy-start(bf16[1,128,16,128]{3,2,1,0:T(8,128)(2,1)} %param.14) | copy-start | bytes 1572868
  558.2 22.5 %copy-start.4 = (f32[128,16,64]{0,2,1:T(8,128)S(1)}, f32[128,16,64]{0,2,1:T(8,128)}, u32[]{:S(2)}) copy-start(f32[128,16,64]{0,2,1:T(8,128)} %copy-done.3) | copy-start | bytes 1572868
  558.2 22.5 %copy-start.6 = (f32[128,16,64]{0,2,1:T(8,128)S(1)}, f32[128,16,64]{0,2,1:T(8,128)}, u32[]{:S(2)}) copy-start(f32[128,16,64]{0,2,1:T(8,128)} %copy-done.5) | copy-start | bytes 1572868
  558.2 22.8 %copy-start.2 = (bf16[128,2,8,128]{3,0,2,1:T(8,128)(2,1)S(1)}, bf16[128,2,8,128]{3,0,2,1:T(8,128)(2,1)}, u32[]{:S(2)}) copy-start(bf16[128,2,8,128]{3,0,2,1:T(8,128)(2,1)} %copy-done.1) | copy-start | bytes 1572868
Sparse Core Ops, SparseCore 0:
  10.1 75.7 all-gather.8
  88.0 71.9 all-gather.10
  162.6 185.8 all-gather.12
  354.4 203.6 all-gather.14
  582.6 1193.7 all-reduce.2
where the time goes:
time: 1790 us
  waiting for transfers between devices  1280 us (72%)
  blocking collectives  395 us (22%)
  local copies, waits for them, and re-layouts  37.4 us (2%)
  matrix products  29.6 us (2%)
  other arithmetic  23.4 us (1%)
    psum x1, waiting for transfers between devices, shards(): lax.psum((query_map_gradient, key_map_gradient, loss_part), ('dp', 'ctx'))  890 us
    psum x1, blocking collectives, shards(): lax.psum((query_map_gradient, key_map_gradient, loss_part), ('dp', 'ctx'))  304 us
    all_gather x2, waiting for transfers between devices, entering(): lax.all_gather(a.astype(kind), axis)  286 us
    all_gather x2, blocking collectives, entering(): lax.all_gather(a.astype(kind), axis)  90.8 us
    all_gather x1, waiting for transfers between devices, shards(): value_piece = lax.all_gather(values, 'ctx', axis=1, tiled=True)[0]  74.1 us
  transfers between devices with their start and end apart: 5, of which 5 were waited for; matrix products, arithmetic and copies ran while one was open for 3% of the time, Pallas kernels for 0%

commit v1 on v0

v1 whole, which is shorter than its diff:
```python
import functools
import math

import jax
import jax.numpy as jnp
from jax import lax
from jax.experimental import pallas as pl
from jax.experimental.pallas import tpu as pltpu
from jax.sharding import PartitionSpec as P

F32 = jnp.float32
BF16 = jnp.bfloat16
CHUNK = 256
LOSS_ROWS = 16


def nn(left, right):
    return lax.dot_general(left, right, (((1,), (0,)), ((), ())), preferred_element_type=F32)


def nt(left, right):
    return lax.dot_general(left, right, (((1,), (1,)), ((), ())), preferred_element_type=F32)


def halves(array):
    high = array.astype(BF16)
    return high, (array - high.astype(F32)).astype(BF16)


def wide_nn(left, right):
    rows = left.shape[0]
    both = nn(jnp.concatenate(halves(left), 0), right)
    return both[:rows] + both[rows:]


def sort_rows(groups):
    rows = 256
    span = rows // groups
    to = lax.broadcasted_iota(jnp.int32, (rows, rows), 0)
    source = lax.broadcasted_iota(jnp.int32, (rows, rows), 1)
    wanted = lax.rem(to, span) * groups + lax.div(to, span)
    return (source == wanted).astype(F32).astype(BF16)


def pack_kernel(q_ref, k_ref, v_ref, out_ref):
    heads = out_ref.shape[0]
    tokens = out_ref.shape[1] // 3
    value_heads = k_ref.shape[0] // tokens
    group = heads // value_heads
    span = 256 // heads
    order = sort_rows(heads)
    for step in range(tokens // span):
        rows = nn(order, q_ref[step * 256 : (step + 1) * 256, :]).astype(BF16)
        out_ref[:, step * span : (step + 1) * span, :] = rows.reshape(heads, span, rows.shape[-1])
    order = sort_rows(value_heads)
    span = 256 // value_heads
    for place, ref in ((tokens, k_ref), (2 * tokens, v_ref)):
        for step in range(tokens // span):
            rows = nn(order, ref[step * 256 : (step + 1) * 256, :]).astype(BF16)
            start = place + step * span
            for head in range(heads):
                own = head // group
                out_ref[head, start : start + span, :] = rows[own * span : (own + 1) * span, :]


def feature_halves(inputs, mapping_t):
    logits = nt(mapping_t, inputs)
    positive = jnp.exp(logits - jnp.max(logits, 0, keepdims=True))
    negative = jnp.exp(jnp.min(logits, 0, keepdims=True) - logits)
    positive = positive / jnp.sum(positive, 0, keepdims=True)
    negative = negative / jnp.sum(negative, 0, keepdims=True)
    return positive, negative


def logit_gradient(positive, negative, gradient):
    half = positive.shape[0]
    up = gradient[:half]
    down = gradient[half:]
    up = positive * (up - jnp.sum(up * positive, 0, keepdims=True))
    down = negative * (down - jnp.sum(down * negative, 0, keepdims=True))
    return up - down


def head_kernel(token_count, x_ref, mq_ref, mk_ref, out_ref, kp, kn, qf, w_ref, g_ref):
    blocks, rows3, size = x_ref.shape
    tokens = rows3 // 3
    per = CHUNK // tokens
    chunks = blocks // per
    feat = mq_ref.shape[-1]
    scale = size**-0.5 * math.log2(math.e)
    mq_t = mq_ref[...].astype(F32).T.astype(BF16)
    mk_t = mk_ref[...].astype(F32).T.astype(BF16)

    def part(which, first, last):
        piece = x_ref[first * per : last * per, which * tokens : (which + 1) * tokens, :]
        return piece.reshape((last - first) * CHUNK, size)

    row = lax.broadcasted_iota(jnp.int32, (CHUNK, CHUNK), 0)
    col = lax.broadcasted_iota(jnp.int32, (CHUNK, CHUNK), 1)
    causal = row >= col
    state = jnp.zeros((2 * feat, 2 * size), F32)
    query_map = jnp.zeros((feat, size), F32)
    loss = jnp.zeros((CHUNK, size), F32)
    for c in range(chunks):
        q = part(0, c, c + 1)
        k = part(1, c, c + 1)
        v = part(2, c, c + 1)
        last = jnp.where(causal, nt(q, k), -jnp.inf)
        peak = jnp.max(last, -1, keepdims=True)
        if c:
            first = nt(q, part(1, 0, c))
            peak = jnp.maximum(peak, jnp.max(first, -1, keepdims=True))
        expo = jnp.exp2((last - peak) * scale)
        mass = jnp.sum(expo, -1, keepdims=True)
        target = nn(expo.astype(BF16), v)
        if c:
            expo = jnp.exp2((first - peak) * scale)
            mass = mass + jnp.sum(expo, -1, keepdims=True)
            target = target + nn(expo.astype(BF16), part(2, 0, c))
        target = target / mass
        q_up, q_down = feature_halves(q, mq_t)
        k_up, k_down = feature_halves(k, mk_t)
        kp[c] = k_up
        kn[c] = k_down
        q_joined = jnp.concatenate([q_up, q_down], 0)
        phi_qt = q_joined.astype(BF16)
        phi_q = q_joined.T.astype(BF16)
        phi_kt = jnp.concatenate([k_up, k_down], 0).astype(BF16)
        qf[c] = phi_qt
        v_wide = jnp.concatenate([v, jnp.ones_like(v)], 1)
        scores = jnp.where(causal, nn(phi_q, phi_kt), 0.0)
        score_high, score_low = halves(scores)
        state_low = state.astype(BF16)
        summed = nn(score_high, v_wide) + nn(score_low, v_wide) + nn(phi_q, state_low)
        inverse = 1.0 / summed[:, size:]
        student = summed[:, :size] * inverse
        residual = student - target
        loss = loss + residual * residual
        gradient = residual * inverse * (2.0 / token_count)
        wide = jnp.concatenate([gradient, -gradient * student], 1).astype(BF16)
        g_ref[c] = wide
        weights = jnp.where(causal, nt(wide, v_wide), 0.0).astype(BF16)
        w_ref[c] = weights
        q_gradient = nt(phi_kt, weights) + nt(state_low, wide)
        state = state + nn(phi_kt, v_wide)
        query_map = query_map + wide_nn(logit_gradient(q_up, q_down, q_gradient), q)
    suffix = jnp.zeros((2 * feat, 2 * size), F32)
    key_map = jnp.zeros((feat, size), F32)
    for c in reversed(range(chunks)):
        k = part(1, c, c + 1)
        v = part(2, c, c + 1)
        v_wide = jnp.concatenate([v, jnp.ones_like(v)], 1)
        phi_qt = qf[c]
        k_gradient = nn(phi_qt, w_ref[c]) + nt(suffix.astype(BF16), v_wide)
        suffix = suffix + nn(phi_qt, g_ref[c])
        key_map = key_map + wide_nn(logit_gradient(kp[c], kn[c], k_gradient), k)
    maps = jnp.concatenate([query_map, key_map], 0).T
    out_ref[0:size, :] = maps.astype(BF16)
    total = jnp.sum(jnp.sum(loss, 0, keepdims=True), 1, keepdims=True) * (1.0 / token_count)
    out_ref[size:, :] = loss_rows(total)


def loss_rows(total):
    high = jnp.broadcast_to(total, (LOSS_ROWS, 128)).astype(BF16).astype(F32)
    low = total - high
    row = lax.broadcasted_iota(jnp.int32, (LOSS_ROWS, 128), 0)
    return jnp.where(row == 0, high, jnp.where(row == 1, low, 0.0)).astype(BF16)


def add_kernel(x_ref, out_ref):
    size = x_ref.shape[1] - LOSS_ROWS
    total = x_ref[0].astype(F32)
    for place in range(1, x_ref.shape[0]):
        total = total + x_ref[place].astype(F32)
    maps = total[:size].astype(BF16)
    loss = loss_rows(total[size : size + 1, 0:1] + total[size + 1 : size + 2, 0:1])
    for place in range(out_ref.shape[0]):
        out_ref[place, 0:size, :] = maps
        out_ref[place, size:, :] = loss


def spread_kernel(x_ref, query_ref, key_ref, loss_ref):
    size = query_ref.shape[1]
    feat = query_ref.shape[2]
    for head in range(x_ref.shape[0]):
        maps = x_ref[head, 0:size, :].astype(F32)
        query_ref[head] = maps[:, :feat]
        key_ref[head] = maps[:, feat:]
        tail = x_ref[head, size:, :].astype(F32)
        loss_ref[head : head + 1, :] = tail[0:1, :] + tail[1:2, :]


VMEM = pl.BlockSpec(memory_space=pltpu.VMEM)


def call(kernel, shapes, inputs, scratch=(), limit=32):
    many = isinstance(shapes, (list, tuple))
    return pl.pallas_call(
        kernel,
        out_shape=shapes,
        in_specs=[VMEM] * len(inputs),
        out_specs=[VMEM] * len(shapes) if many else VMEM,
        scratch_shapes=list(scratch),
        compiler_params=pltpu.CompilerParams(vmem_limit_bytes=limit * 2**20),
    )(*inputs)


def shards(queries, keys, values, map_query, map_key):
    _, tokens, heads, size = queries.shape
    feat = map_query.shape[-1]
    dp = lax.axis_size("dp")
    ctx = lax.axis_size("ctx")
    token_count = dp * ctx * tokens
    shape = jax.ShapeDtypeStruct
    packed = call(
        pack_kernel,
        shape((heads, 3 * tokens, size), BF16),
        [queries.reshape(-1, size), keys.reshape(-1, size), values.reshape(-1, size)],
    )
    mine = lax.axis_index("ctx")
    own_query = lax.dynamic_index_in_dim(map_query, mine, 0, False)
    own_key = lax.dynamic_index_in_dim(map_key, mine, 0, False)
    sequence = lax.all_to_all(packed, "ctx", 0, 0, tiled=True)
    chunks = ctx * tokens // CHUNK
    part = call(
        functools.partial(head_kernel, token_count),
        shape((size + LOSS_ROWS, size), BF16),
        [sequence, own_query, own_key],
        [
            pltpu.VMEM((chunks, feat, CHUNK), F32),
            pltpu.VMEM((chunks, feat, CHUNK), F32),
            pltpu.VMEM((chunks, 2 * feat, CHUNK), BF16),
            pltpu.VMEM((chunks, CHUNK, CHUNK), BF16),
            pltpu.VMEM((chunks, CHUNK, 2 * size), BF16),
        ],
        48,
    )
    parts = jnp.broadcast_to(part[None], (dp,) + part.shape)
    parts = lax.all_to_all(parts, "dp", 0, 0, tiled=True)
    whole = call(add_kernel, shape((ctx,) + part.shape, BF16), [parts])
    gathered = lax.all_to_all(whole, "ctx", 0, 0, tiled=True)
    grad_query, grad_key, loss = call(
        spread_kernel,
        [shape((heads, size, feat), F32), shape((heads, size, feat), F32), shape((heads, size), F32)],
        [gathered],
    )
    return grad_query, grad_key, loss[:, 0]


def solution(mesh):
    placed = P("dp", "ctx", "head", None)
    maps = P("head", None, None)
    return jax.shard_map(
        shards,
        mesh=mesh,
        in_specs=(placed, placed, placed, maps, maps),
        out_specs=(maps, maps, P("head")),
        check_vma=False,
    )
```

time: 1790 us -> 114 us (0.06)
  waiting for transfers between devices: 1280 us -> 38.6 us
  blocking collectives: 395 us -> 43.8 us
  local copies, waits for them, and re-layouts: 37.4 us -> 6.58 us
  matrix products: 29.6 us -> 0 us
  other arithmetic: 23.4 us -> 0 us
    psum x1 -> x0, waiting for transfers between devices: 890 us -> none  [shards(): lax.psum((query_map_gradient, key_map_gradient, loss_part), ('dp', 'ctx'))]
    all_gather x4 -> x0, waiting for transfers between devices: 386 us -> none  [the longest x2 286 us: entering(): lax.all_gather(a.astype(kind), axis)]
    psum x1 -> x0, blocking collectives: 304 us -> none  [shards(): lax.psum((query_map_gradient, key_map_gradient, loss_part), ('dp', 'ctx'))]
    all_gather x2 -> x0, blocking collectives: 90.8 us -> none  [entering(): lax.all_gather(a.astype(kind), axis)]
    all_to_all x0 -> x2, blocking collectives: none -> 43.8 us  [the longest x1 22.9 us: shards(): gathered = lax.all_to_all(whole, 'ctx', 0, 0, tiled=True)]
    all_to_all x0 -> x1, waiting for transfers between devices: none -> 38.6 us  [shards(): sequence = lax.all_to_all(packed, 'ctx', 0, 0, tiled=True)]
    dot_general x16 -> x0, matrix products: 22.2 us -> none  [the longest x12 19.8 us: precise(): jnp.einsum(pattern, left_side, right_side, precision=HIGH, preferred_elem...]
    add x33 -> x0, other arithmetic: 19.5 us -> none  [the longest x30 19.5 us: combine_sum(): return jax.tree.map(jnp.add, earlier, later_part)]
  transfers between devices with their start and end apart: 5 -> 1, of which waited for: 5 -> 1; matrix products, arithmetic and copies ran while one was open for 3% -> 1% of each run, Pallas kernels for 0% -> 0%
where the time goes in v1:
time: 114 us
  blocking collectives  43.8 us (38%)
  waiting for transfers between devices  38.6 us (34%)
  Pallas kernels  16.1 us (14%)
  starting transfers between devices  7.84 us (7%)
  local copies, waits for them, and re-layouts  6.58 us (6%)
    all_to_all x1, waiting for transfers between devices, shards(): sequence = lax.all_to_all(packed, 'ctx', 0, 0, tiled=True)  38.6 us
    all_to_all x1, blocking collectives, shards(): gathered = lax.all_to_all(whole, 'ctx', 0, 0, tiled=True)  22.9 us
    all_to_all x1, blocking collectives, shards(): parts = lax.all_to_all(parts, 'dp', 0, 0, tiled=True)  20.9 us
    pallas_call x4, Pallas kernels, call(): pl.pallas_call(kernel, out_shape=shapes, in_specs=[VMEM] * len(inputs), o...  16.1 us
    all_to_all x1, starting transfers between devices, shards(): sequence = lax.all_to_all(packed, 'ctx', 0, 0, tiled=True)  7.84 us
    unnamed x8, local copies, waits for them, and re-layouts  4.94 us
  transfers between devices with their start and end apart: 1, of which 1 were waited for; matrix products, arithmetic and copies ran while one was open for 1% of the time, Pallas kernels for 0%

profile of v1, /device:TPU:4, one launch (start us, length us, event | category | flops | bytes accessed | tf_op | source)
XLA Modules:
  0.0 113.6 jit_solution(15936338038107171601)
XLA Ops:
  0.6 0.0 copy-start
  0.6 1.0 copy-done
  1.7 0.0 copy-start.1
  1.7 0.8 copy-done.1
  2.5 0.0 copy-start.2
  2.5 0.8 copy-done.2
  3.4 1.7 %shard_map.76 = bf16[16,384,128]{2,1,0:T(8,128)(2,1)} custom-call(bf16[2048,128]{1,0:T(8,128)(2,1)S(1)} %bitcast.5, bf16[256,128]{1,0:T(8,128)(2,1)S(1)} %bitcast.8, bf16[256,128]{1,0:T(8,128)(2,1)S(1)} %bitcast.9), custom_call_target="tpu_custom_call" | custom-call | tf_op jit(solution)/shard_map/pallas_call | solution.py:198
  5.0 7.8 %all-to-all-start = ((bf16[16,384,128]{2,1,0:T(8,128)(2,1)}), bf16[16,384,128]{2,1,0:T(8,128)(2,1)S(1)}, u32[]{:S(2)}, u32[]{:S(2)}) async-start(bf16[16,384,128]{2,1,0:T(8,128)(2,1)} %shard_map.76), calls=%async_computation | async-start | bytes 3145728 | tf_op jit(solution)/shard_map/all_to_all | solution.py:223
  12.9 0.7 constant_dynamic-slice_fusion
  13.6 0.1 copy.12
  13.8 0.1 copy.13
  13.9 38.6 %all-to-all-done.x_ref = bf16[16,384,128]{2,1,0:T(8,128)(2,1)S(1)} async-done(((bf16[16,384,128]{2,1,0:T(8,128)(2,1)}), bf16[16,384,128]{2,1,0:T(8,128)(2,1)S(1)}, u32[]{:S(2)}, u32[]{:S(2)}) %all-to-all-start) | async-done | bytes 1572896 | tf_op jit(solution)/shard_map/all_to_all | solution.py:223
  52.5 14.1 %shard_map.77 = bf16[144,128]{1,0:T(8,128)(2,1)S(1)} custom-call(bf16[16,384,128]{2,1,0:T(8,128)(2,1)S(1)} %all-to-all-done.x_ref, bf16[128,64]{1,0:T(8,128)(2,1)S(1)} %bitcast.6, bf16[128,64]{1,0:T(8,128)(2,1)S(1)} %bitcast.7), custom_call_target="tpu_custom_call" | custom-call | tf_op jit(solution)/shard_map/pallas_call | solution.py:198
  66.6 20.9 %all_to_all.15.x_ref = bf16[8,144,128]{2,1,0:T(8,128)(2,1)S(1)} all-to-all(bf16[8,144,128]{2,1,0:T(8,128)(2,1)S(1)} %broadcast_in_dim.2), channel_id=1, replica_groups=mesh['dp'=8,'ctx'=16,'head'=4] {'dp'}, dimensions={0} | all-to-all | bytes 589824 | tf_op jit(solution)/shard_map/all_to_all | solution.py:239
  87.6 0.1 shard_map.78
  87.7 22.9 %all_to_all.16.x_ref = bf16[16,144,128]{2,1,0:T(8,128)(2,1)S(1)} all-to-all(bf16[16,144,128]{2,1,0:T(8,128)(2,1)S(1)} %shard_map.78), channel_id=1, replica_groups=mesh['dp'=8,'ctx'=16,'head'=4] {'ctx'}, dimensions={0} | all-to-all | bytes 1179648 | tf_op jit(solution)/shard_map/all_to_all | solution.py:241
  110.6 0.2 shard_map.79
  110.8 1.1 copy.14
  111.9 1.1 copy.15
  113.0 0.6 slice_reduce_fusion
  (1 shorter events, 0.0 us)
Async XLA Ops:
  0.6 1.0 copy-start
  1.7 0.8 copy-start.1
  2.5 0.8 copy-start.2
  5.0 47.4 %all-to-all-start = ((bf16[16,384,128]{2,1,0:T(8,128)(2,1)}), bf16[16,384,128]{2,1,0:T(8,128)(2,1)S(1)}, u32[]{:S(2)}, u32[]{:S(2)}) async-start(bf16[16,384,128]{2,1,0:T(8,128)(2,1)} %shard_map.76), calls=%async_computation | async-start | bytes 3145728 | tf_op jit(solution)/shard_map/all_to_all | solution.py:223

commit v2 on v1

v2 whole, which is shorter than its diff:
```python
import functools
import math

import jax
import jax.numpy as jnp
from jax import lax
from jax.experimental import pallas as pl
from jax.experimental.pallas import tpu as pltpu
from jax.sharding import PartitionSpec as P

F32 = jnp.float32
BF16 = jnp.bfloat16
CHUNK = 256
LOSS_ROWS = 16


def nn(left, right):
    return lax.dot_general(left, right, (((1,), (0,)), ((), ())), preferred_element_type=F32)


def nt(left, right):
    return lax.dot_general(left, right, (((1,), (1,)), ((), ())), preferred_element_type=F32)


def halves(array):
    high = array.astype(BF16)
    return high, (array - high.astype(F32)).astype(BF16)


def wide_nn(left, right):
    rows = left.shape[0]
    both = nn(jnp.concatenate(halves(left), 0), right)
    return both[:rows] + both[rows:]


def sort_rows(groups):
    rows = 256
    span = rows // groups
    shift = span.bit_length() - 1
    to = lax.broadcasted_iota(jnp.int32, (rows, rows), 0)
    source = lax.broadcasted_iota(jnp.int32, (rows, rows), 1)
    wanted = (to & (span - 1)) * groups + (to >> shift)
    return (source == wanted).astype(F32).astype(BF16)


def pack_kernel(q_hbm, k_hbm, v_hbm, out_ref, q_ref, k_ref, v_ref, sems):
    copies = [
        pltpu.make_async_copy(source, target, sems.at[place])
        for place, (source, target) in enumerate(((k_hbm, k_ref), (v_hbm, v_ref), (q_hbm, q_ref)))
    ]
    for copy in copies:
        copy.start()
    heads = out_ref.shape[0]
    tokens = out_ref.shape[1] // 3
    value_heads = k_ref.shape[0] // tokens
    group = heads // value_heads
    order = sort_rows(heads)
    value_order = sort_rows(value_heads)
    for place, ref in enumerate((k_ref, v_ref)):
        span = 256 // value_heads
        copies[place].wait()
        for step in range(tokens // span):
            rows = nn(value_order, ref[step * 256 : (step + 1) * 256, :]).astype(BF16)
            start = (place + 1) * tokens + step * span
            for head in range(heads):
                own = head // group
                out_ref[head, start : start + span, :] = rows[own * span : (own + 1) * span, :]
    span = 256 // heads
    copies[2].wait()
    for step in range(tokens // span):
        rows = nn(order, q_ref[step * 256 : (step + 1) * 256, :]).astype(BF16)
        out_ref[:, step * span : (step + 1) * span, :] = rows.reshape(heads, span, rows.shape[-1])


def feature_halves(inputs, mapping_t):
    logits = nt(mapping_t, inputs)
    positive = jnp.exp(logits - jnp.max(logits, 0, keepdims=True))
    negative = jnp.exp(jnp.min(logits, 0, keepdims=True) - logits)
    positive = positive / jnp.sum(positive, 0, keepdims=True)
    negative = negative / jnp.sum(negative, 0, keepdims=True)
    return positive, negative


def logit_gradient(positive, negative, gradient):
    half = positive.shape[0]
    up = gradient[:half]
    down = gradient[half:]
    up = positive * (up - jnp.sum(up * positive, 0, keepdims=True))
    down = negative * (down - jnp.sum(down * negative, 0, keepdims=True))
    return up - down


def head_kernel(token_count, x_ref, mq_ref, mk_ref, out_ref):
    blocks, rows3, size = x_ref.shape
    tokens = rows3 // 3
    per = CHUNK // tokens
    chunks = range(blocks // per)
    feat = mq_ref.shape[0]
    scale = size**-0.5 * math.log2(math.e)

    def part(which, first, last):
        piece = x_ref[first * per : last * per, which * tokens : (which + 1) * tokens, :]
        return piece.reshape((last - first) * CHUNK, size)

    def each(make):
        return [make(c) for c in chunks]

    row = lax.broadcasted_iota(jnp.int32, (CHUNK, CHUNK), 0)
    col = lax.broadcasted_iota(jnp.int32, (CHUNK, CHUNK), 1)
    causal = row >= col
    q = each(lambda c: part(0, c, c + 1))
    k = each(lambda c: part(1, c, c + 1))
    ones = jnp.ones((CHUNK, size), BF16)
    v_wide = each(lambda c: jnp.concatenate([part(2, c, c + 1), ones], 1))
    mq_t = mq_ref[...]
    mk_t = mk_ref[...]

    k_up, k_down = zip(*each(lambda c: feature_halves(k[c], mk_t)))
    q_up, q_down = zip(*each(lambda c: feature_halves(q[c], mq_t)))
    phi_kt = each(lambda c: jnp.concatenate([k_up[c], k_down[c]], 0).astype(BF16))
    q_joined = each(lambda c: jnp.concatenate([q_up[c], q_down[c]], 0))
    phi_qt = each(lambda c: q_joined[c].astype(BF16))
    phi_q = each(lambda c: q_joined[c].T.astype(BF16))
    state = [jnp.zeros((2 * feat, 2 * size), F32)]
    for c in chunks[:-1]:
        state.append(state[-1] + nn(phi_kt[c], v_wide[c]))
    state_low = each(lambda c: state[c].astype(BF16))
    scores = each(lambda c: halves(jnp.where(causal, nn(phi_q[c], phi_kt[c]), 0.0)))

    def teacher(c):
        last = jnp.where(causal, nt(q[c], k[c]), -jnp.inf)
        peak = jnp.max(last, -1, keepdims=True)
        if c:
            first = nt(q[c], part(1, 0, c))
            peak = jnp.maximum(peak, jnp.max(first, -1, keepdims=True))
        expo = jnp.exp2((last - peak) * scale)
        mass = jnp.sum(expo, -1, keepdims=True)
        target = nn(expo.astype(BF16), part(2, c, c + 1))
        if c:
            expo = jnp.exp2((first - peak) * scale)
            mass = mass + jnp.sum(expo, -1, keepdims=True)
            target = target + nn(expo.astype(BF16), part(2, 0, c))
        return target / mass

    target = each(teacher)
    summed = each(
        lambda c: nn(scores[c][0], v_wide[c]) + nn(scores[c][1], v_wide[c]) + nn(phi_q[c], state_low[c])
    )
    loss = jnp.zeros((CHUNK, size), F32)
    wide = []
    for c in chunks:
        inverse = 1.0 / summed[c][:, size:]
        student = summed[c][:, :size] * inverse
        residual = student - target[c]
        loss = loss + residual * residual
        gradient = residual * inverse * (2.0 / token_count)
        wide.append(jnp.concatenate([gradient, -gradient * student], 1).astype(BF16))
    suffix = [jnp.zeros((2 * feat, 2 * size), F32)]
    for c in reversed(chunks[1:]):
        suffix.insert(0, suffix[0] + nn(phi_qt[c], wide[c]))
    weights = each(lambda c: halves(jnp.where(causal, nt(wide[c], v_wide[c]), 0.0)))
    q_gradient = each(
        lambda c: nt(phi_kt[c], weights[c][0]) + nt(phi_kt[c], weights[c][1]) + nt(state_low[c], wide[c])
    )
    k_gradient = each(
        lambda c: nn(phi_qt[c], weights[c][0])
        + nn(phi_qt[c], weights[c][1])
        + nt(suffix[c].astype(BF16), v_wide[c])
    )
    query_map = sum(each(lambda c: wide_nn(logit_gradient(q_up[c], q_down[c], q_gradient[c]), q[c])))
    key_map = sum(each(lambda c: wide_nn(logit_gradient(k_up[c], k_down[c], k_gradient[c]), k[c])))
    maps = jnp.concatenate([query_map, key_map], 0)
    out_ref[0:size, :] = maps.astype(BF16)
    total = jnp.sum(jnp.sum(loss, 0, keepdims=True), 1, keepdims=True) * (1.0 / token_count)
    out_ref[size:, :] = loss_rows(total)


def loss_rows(total):
    high = jnp.broadcast_to(total, (LOSS_ROWS, 128)).astype(BF16).astype(F32)
    low = total - high
    row = lax.broadcasted_iota(jnp.int32, (LOSS_ROWS, 128), 0)
    return jnp.where(row == 0, high, jnp.where(row == 1, low, 0.0)).astype(BF16)


def add_kernel(x_ref, out_ref):
    size = x_ref.shape[1] - LOSS_ROWS
    total = x_ref[0].astype(F32)
    for place in range(1, x_ref.shape[0]):
        total = total + x_ref[place].astype(F32)
    maps = total[:size].astype(BF16)
    loss = loss_rows(total[size : size + 1, 0:1] + total[size + 1 : size + 2, 0:1])
    for place in range(out_ref.shape[0]):
        out_ref[place, 0:size, :] = maps
        out_ref[place, size:, :] = loss


def spread_kernel(x_ref, query_hbm, key_hbm, loss_ref, query_ref, key_ref, sems):
    heads, feat, _ = query_ref.shape
    size = 2 * feat
    parts = sems.shape[1]
    each = heads // parts
    lane = lax.broadcasted_iota(jnp.int32, (1, heads), 1)
    loss = jnp.zeros((1, heads), F32)
    copies = []
    for part in range(parts):
        own = pl.ds(part * each, each)
        for head in range(part * each, (part + 1) * each):
            query_ref[head] = x_ref[head, 0:feat, :].astype(F32)
            key_ref[head] = x_ref[head, feat:size, :].astype(F32)
        for place, (source, target) in enumerate(((query_ref, query_hbm), (key_ref, key_hbm))):
            copies.append(pltpu.make_async_copy(source.at[own], target.at[own], sems.at[place, part]))
            copies[-1].start()
    for head in range(heads):
        tail = x_ref[head, size:, :].astype(F32)
        loss = jnp.where(lane == head, tail[0:1, :heads] + tail[1:2, :heads], loss)
    loss_ref[...] = loss
    for copy in copies:
        copy.wait()


VMEM = pl.BlockSpec(memory_space=pltpu.VMEM)


HBM = pl.BlockSpec(memory_space=pltpu.HBM)


def call(kernel, shapes, inputs, scratch=(), limit=32, in_specs=None, out_specs=VMEM):
    return pl.pallas_call(
        kernel,
        out_shape=shapes,
        in_specs=in_specs or [VMEM] * len(inputs),
        out_specs=out_specs,
        scratch_shapes=list(scratch),
        compiler_params=pltpu.CompilerParams(vmem_limit_bytes=limit * 2**20),
    )(*inputs)


def head_call(sequence, own_query, own_key, token_count):
    blocks, rows, size = sequence.shape
    chunks = blocks * rows // 3 // CHUNK
    return call(
        functools.partial(head_kernel, token_count),
        jax.ShapeDtypeStruct((size + LOSS_ROWS, size), BF16),
        [sequence, own_query, own_key],
        (),
        48,
    )


def shards(queries, keys, values, map_query, map_key):
    _, tokens, heads, size = queries.shape
    feat = map_query.shape[-1]
    dp = lax.axis_size("dp")
    ctx = lax.axis_size("ctx")
    token_count = dp * ctx * tokens
    shape = jax.ShapeDtypeStruct
    rows = [
        pltpu.with_memory_space_constraint(array.reshape(-1, size), pltpu.HBM)
        for array in (queries, keys, values)
    ]
    packed = call(
        pack_kernel,
        shape((heads, 3 * tokens, size), BF16),
        rows,
        [pltpu.VMEM(array.shape, BF16) for array in rows] + [pltpu.SemaphoreType.DMA((3,))],
        in_specs=[HBM] * 3,
    )
    mine = lax.axis_index("ctx")
    own_query = lax.dynamic_index_in_dim(jnp.swapaxes(map_query, 1, 2), mine, 0, False)
    own_key = lax.dynamic_index_in_dim(jnp.swapaxes(map_key, 1, 2), mine, 0, False)
    sequence = lax.all_to_all(packed, "ctx", 0, 0, tiled=True)
    part = head_call(sequence, own_query, own_key, token_count)
    parts = jnp.broadcast_to(part[None], (dp,) + part.shape)
    parts = lax.all_to_all(parts, "dp", 0, 0, tiled=True)
    whole = call(add_kernel, shape((ctx,) + part.shape, BF16), [parts])
    gathered = lax.all_to_all(whole, "ctx", 0, 0, tiled=True)
    maps = (heads, feat, size)
    grad_query, grad_key, loss = call(
        spread_kernel,
        [shape(maps, F32), shape(maps, F32), shape((1, heads), F32)],
        [gathered],
        [pltpu.VMEM(maps, F32), pltpu.VMEM(maps, F32), pltpu.SemaphoreType.DMA((2, 2))],
        out_specs=[HBM, HBM, VMEM],
    )
    return jnp.swapaxes(grad_query, 1, 2), jnp.swapaxes(grad_key, 1, 2), loss.reshape(heads)


def solution(mesh):
    placed = P("dp", "ctx", "head", None)
    maps = P("head", None, None)
    return jax.shard_map(
        shards,
        mesh=mesh,
        in_specs=(placed, placed, placed, maps, maps),
        out_specs=(maps, maps, P("head")),
        check_vma=False,
    )
```

time: 114 us -> 106 us (0.930)
  local copies, waits for them, and re-layouts: 6.58 us -> 0.78 us
  Pallas kernels: 16.1 us -> 13.2 us
    unnamed x8 -> x0, local copies, waits for them, and re-layouts: 4.94 us -> none
    pallas_call x4, Pallas kernels: 16.1 us -> 13.2 us  [call(): pl.pallas_call(kernel, out_shape=shapes, in_specs=in_specs or [VMEM] * le...]
where the time goes in v2:
time: 106 us; the launch traced here: 105 us
  blocking collectives  43.8 us (41%)
  waiting for transfers between devices  38.8 us (37%)
  Pallas kernels  13.2 us (12%)
  starting transfers between devices  7.85 us (7%)
    all_to_all x1, waiting for transfers between devices, shards(): sequence = lax.all_to_all(packed, 'ctx', 0, 0, tiled=True)  38.8 us
    all_to_all x1, blocking collectives, shards(): gathered = lax.all_to_all(whole, 'ctx', 0, 0, tiled=True)  22.9 us
    all_to_all x1, blocking collectives, shards(): parts = lax.all_to_all(parts, 'dp', 0, 0, tiled=True)  21 us
    pallas_call x4, Pallas kernels, call(): pl.pallas_call(kernel, out_shape=shapes, in_specs=in_specs or [VMEM] * le...  13.2 us
    all_to_all x1, starting transfers between devices, shards(): sequence = lax.all_to_all(packed, 'ctx', 0, 0, tiled=True)  7.85 us
  transfers between devices with their start and end apart: 1, of which 1 were waited for; matrix products, arithmetic and copies ran while one was open for 1% of the time, Pallas kernels for 0%

profile of v2, /device:TPU:4, one launch (start us, length us, event | category | flops | bytes accessed | tf_op | source)
XLA Modules:
  0.0 105.2 jit_solution(15188196421340662931)
XLA Ops:
  0.6 2.9 %shard_map.76 = bf16[16,384,128]{2,1,0:T(8,128)(2,1)} custom-call(bf16[2048,128]{1,0:T(8,128)(2,1)} %bitcast.14, bf16[256,128]{1,0:T(8,128)(2,1)} %bitcast.15, bf16[256,128]{1,0:T(8,128)(2,1)} %bitcast.16), custom_call_target="tpu_custom_call" | custom-call | tf_op jit(solution)/shard_map/pallas_call | solution.py:228
  3.5 7.9 %all-to-all-start = ((bf16[16,384,128]{2,1,0:T(8,128)(2,1)}), bf16[16,384,128]{2,1,0:T(8,128)(2,1)S(1)}, u32[]{:S(2)}, u32[]{:S(2)}) async-start(bf16[16,384,128]{2,1,0:T(8,128)(2,1)} %shard_map.76), calls=%async_computation | async-start | bytes 3145728 | tf_op jit(solution)/shard_map/all_to_all | solution.py:271
  11.4 0.7 dynamic-slice_bitcast_fusion
  12.1 38.8 %all-to-all-done.x_ref = bf16[16,384,128]{2,1,0:T(8,128)(2,1)S(1)} async-done(((bf16[16,384,128]{2,1,0:T(8,128)(2,1)}), bf16[16,384,128]{2,1,0:T(8,128)(2,1)S(1)}, u32[]{:S(2)}, u32[]{:S(2)}) %all-to-all-start) | async-done | bytes 1572896 | tf_op jit(solution)/shard_map/all_to_all | solution.py:271
  51.0 8.7 %shard_map.77 = bf16[144,128]{1,0:T(8,128)(2,1)S(1)} custom-call(bf16[16,384,128]{2,1,0:T(8,128)(2,1)S(1)} %all-to-all-done.x_ref, bf16[64,128]{1,0:T(8,128)(2,1)S(1)} %get-tuple-element.10.mq_ref, bf16[64,128]{1,0:T(8,128)(2,1)S(1)} %get-tuple-element.9.mk_ref), custom_call_target="tpu_custom_call" | custom-call | tf_op jit(solution)/shard_map/pallas_call | solution.py:228
  59.7 21.0 %all_to_all.15.x_ref = bf16[8,144,128]{2,1,0:T(8,128)(2,1)S(1)} all-to-all(bf16[8,144,128]{2,1,0:T(8,128)(2,1)S(1)} %broadcast_in_dim.2), channel_id=1, replica_groups=mesh['dp'=8,'ctx'=16,'head'=4] {'dp'}, dimensions={0} | all-to-all | bytes 589824 | tf_op jit(solution)/shard_map/all_to_all | solution.py:274
  80.7 0.1 shard_map.78
  80.8 22.9 %all_to_all.16.x_ref = bf16[16,144,128]{2,1,0:T(8,128)(2,1)S(1)} all-to-all(bf16[16,144,128]{2,1,0:T(8,128)(2,1)S(1)} %shard_map.78), channel_id=1, replica_groups=mesh['dp'=8,'ctx'=16,'head'=4] {'ctx'}, dimensions={0} | all-to-all | bytes 1179648 | tf_op jit(solution)/shard_map/all_to_all | solution.py:276
  103.7 1.5 %shard_map.79 = (f32[16,64,128]{2,1,0:T(8,128)}, f32[16,64,128]{2,1,0:T(8,128)}, f32[1,16]{1,0:T(1,128)}) custom-call(bf16[16,144,128]{2,1,0:T(8,128)(2,1)S(1)} %all_to_all.16.x_ref), custom_call_target="tpu_custom_call" | custom-call | tf_op jit(solution)/shard_map/pallas_call | solution.py:228
  (1 shorter events, 0.0 us)
Async XLA Ops:
  3.5 47.5 %all-to-all-start = ((bf16[16,384,128]{2,1,0:T(8,128)(2,1)}), bf16[16,384,128]{2,1,0:T(8,128)(2,1)S(1)}, u32[]{:S(2)}, u32[]{:S(2)}) async-start(bf16[16,384,128]{2,1,0:T(8,128)(2,1)} %shard_map.76), calls=%async_computation | async-start | bytes 3145728 | tf_op jit(solution)/shard_map/all_to_all | solution.py:271

commit v3 on v2

--- a/solution.py
+++ b/solution.py
@@ -11,7 +11,7 @@
 F32 = jnp.float32
 BF16 = jnp.bfloat16
 CHUNK = 256
-LOSS_ROWS = 16
+LOSS_ROWS = 8
 
 
 def nn(left, right):
@@ -115,34 +115,44 @@
     mq_t = mq_ref[...]
     mk_t = mk_ref[...]
 
-    k_up, k_down = zip(*each(lambda c: feature_halves(k[c], mk_t)))
-    q_up, q_down = zip(*each(lambda c: feature_halves(q[c], mq_t)))
-    phi_kt = each(lambda c: jnp.concatenate([k_up[c], k_down[c]], 0).astype(BF16))
-    q_joined = each(lambda c: jnp.concatenate([q_up[c], q_down[c]], 0))
-    phi_qt = each(lambda c: q_joined[c].astype(BF16))
-    phi_q = each(lambda c: q_joined[c].T.astype(BF16))
+    def feature(c):
+        k_halves = feature_halves(k[c], mk_t)
+        q_halves = feature_halves(q[c], mq_t)
+        q_joined = jnp.concatenate(q_halves, 0)
+        phi_kt = jnp.concatenate(k_halves, 0).astype(BF16)
+        return k_halves, q_halves, phi_kt, q_joined.astype(BF16), q_joined.T.astype(BF16)
+
+    def block(c):
+        last = jnp.where(causal, nt(q[c], k[c]), -jnp.inf)
+        if not c:
+            return (last,)
+        return nt(q[c], part(1, 0, c)), last
+
+    def peak(c):
+        return functools.reduce(jnp.maximum, [jnp.max(s, -1, keepdims=True) for s in blocks_of[c]])
+
+    def teacher(c):
+        expos = [jnp.exp2((s - peaks[c]) * scale) for s in blocks_of[c]]
+        mass = sum(jnp.sum(e, -1, keepdims=True) for e in expos)
+        target = nn(expos[-1].astype(BF16), part(2, c, c + 1))
+        if c:
+            target = target + nn(expos[0].astype(BF16), part(2, 0, c))
+        return target / mass
+
+    def score(c):
+        return halves(jnp.where(causal, nn(phi_q[c], phi_kt[c]), 0.0))
+
+    blocks_of = each(block)
+    peaks = each(peak)
+    made, target = zip(*each(lambda c: (feature(c), teacher(c))))
+    k_halves, q_halves, phi_kt, phi_qt, phi_q = zip(*made)
+    k_up, k_down = zip(*k_halves)
+    q_up, q_down = zip(*q_halves)
     state = [jnp.zeros((2 * feat, 2 * size), F32)]
     for c in chunks[:-1]:
         state.append(state[-1] + nn(phi_kt[c], v_wide[c]))
     state_low = each(lambda c: state[c].astype(BF16))
-    scores = each(lambda c: halves(jnp.where(causal, nn(phi_q[c], phi_kt[c]), 0.0)))
-
-    def teacher(c):
-        last = jnp.where(causal, nt(q[c], k[c]), -jnp.inf)
-        peak = jnp.max(last, -1, keepdims=True)
-        if c:
-            first = nt(q[c], part(1, 0, c))
-            peak = jnp.maximum(peak, jnp.max(first, -1, keepdims=True))
-        expo = jnp.exp2((last - peak) * scale)
-        mass = jnp.sum(expo, -1, keepdims=True)
-        target = nn(expo.astype(BF16), part(2, c, c + 1))
-        if c:
-            expo = jnp.exp2((first - peak) * scale)
-            mass = mass + jnp.sum(expo, -1, keepdims=True)
-            target = target + nn(expo.astype(BF16), part(2, 0, c))
-        return target / mass
-
-    target = each(teacher)
+    scores = each(score)
     summed = each(
         lambda c: nn(scores[c][0], v_wide[c]) + nn(scores[c][1], v_wide[c]) + nn(phi_q[c], state_low[c])
     )
@@ -247,6 +257,34 @@
     )
 
 
+def pack_call(queries, keys, values):
+    _, tokens, heads, size = queries.shape
+    rows = [
+        pltpu.with_memory_space_constraint(array.reshape(-1, size), pltpu.HBM)
+        for array in (queries, keys, values)
+    ]
+    return call(
+        pack_kernel,
+        jax.ShapeDtypeStruct((heads, 3 * tokens, size), BF16),
+        rows,
+        [pltpu.VMEM(array.shape, BF16) for array in rows] + [pltpu.SemaphoreType.DMA((3,))],
+        in_specs=[HBM] * 3,
+    )
+
+
+def spread_call(gathered, feat):
+    heads, rows, size = gathered.shape
+    maps = (heads, feat, size)
+    shape = jax.ShapeDtypeStruct
+    return call(
+        spread_kernel,
+        [shape(maps, F32), shape(maps, F32), shape((1, heads), F32)],
+        [gathered],
+        [pltpu.VMEM(maps, F32), pltpu.VMEM(maps, F32), pltpu.SemaphoreType.DMA((2, 2))],
+        out_specs=[HBM, HBM, VMEM],
+    )
+
+
 def shards(queries, keys, values, map_query, map_key):
     _, tokens, heads, size = queries.shape
     feat = map_query.shape[-1]
@@ -254,17 +292,7 @@
     ctx = lax.axis_size("ctx")
     token_count = dp * ctx * tokens
     shape = jax.ShapeDtypeStruct
-    rows = [
-        pltpu.with_memory_space_constraint(array.reshape(-1, size), pltpu.HBM)
-        for array in (queries, keys, values)
-    ]
-    packed = call(
-        pack_kernel,
-        shape((heads, 3 * tokens, size), BF16),
-        rows,
-        [pltpu.VMEM(array.shape, BF16) for array in rows] + [pltpu.SemaphoreType.DMA((3,))],
-        in_specs=[HBM] * 3,
-    )
+    packed = pack_call(queries, keys, values)
     mine = lax.axis_index("ctx")
     own_query = lax.dynamic_index_in_dim(jnp.swapaxes(map_query, 1, 2), mine, 0, False)
     own_key = lax.dynamic_index_in_dim(jnp.swapaxes(map_key, 1, 2), mine, 0, False)
@@ -274,14 +302,7 @@
     parts = lax.all_to_all(parts, "dp", 0, 0, tiled=True)
     whole = call(add_kernel, shape((ctx,) + part.shape, BF16), [parts])
     gathered = lax.all_to_all(whole, "ctx", 0, 0, tiled=True)
-    maps = (heads, feat, size)
-    grad_query, grad_key, loss = call(
-        spread_kernel,
-        [shape(maps, F32), shape(maps, F32), shape((1, heads), F32)],
-        [gathered],
-        [pltpu.VMEM(maps, F32), pltpu.VMEM(maps, F32), pltpu.SemaphoreType.DMA((2, 2))],
-        out_specs=[HBM, HBM, VMEM],
-    )
+    grad_query, grad_key, loss = spread_call(gathered, feat)
     return jnp.swapaxes(grad_query, 1, 2), jnp.swapaxes(grad_key, 1, 2), loss.reshape(heads)
 
 

time: 106 us -> 103 us (0.972)
  Pallas kernels: 13.2 us -> 11.7 us
    pallas_call x4, Pallas kernels: 13.2 us -> 11.7 us  [call(): pl.pallas_call(kernel, out_shape=shapes, in_specs=in_specs or [VMEM] * le...]
where the time goes in v3:
time: 103 us
  blocking collectives  42.8 us (42%)
  waiting for transfers between devices  38.8 us (38%)
  Pallas kernels  11.7 us (11%)
  starting transfers between devices  7.85 us (8%)
    all_to_all x1, waiting for transfers between devices, shards(): sequence = lax.all_to_all(packed, 'ctx', 0, 0, tiled=True)  38.8 us
    all_to_all x1, blocking collectives, shards(): gathered = lax.all_to_all(whole, 'ctx', 0, 0, tiled=True)  22 us
    all_to_all x1, blocking collectives, shards(): parts = lax.all_to_all(parts, 'dp', 0, 0, tiled=True)  20.8 us
    pallas_call x4, Pallas kernels, call(): pl.pallas_call(kernel, out_shape=shapes, in_specs=in_specs or [VMEM] * le...  11.7 us
    all_to_all x1, starting transfers between devices, shards(): sequence = lax.all_to_all(packed, 'ctx', 0, 0, tiled=True)  7.85 us
  transfers between devices with their start and end apart: 1, of which 1 were waited for; matrix products, arithmetic and copies ran while one was open for 1% of the time, Pallas kernels for 0%

profile of v3, /device:TPU:4, one launch (start us, length us, event | category | flops | bytes accessed | tf_op | source)
XLA Modules:
  0.0 102.6 jit_solution(4804717410929118525)
XLA Ops:
  0.6 2.9 %shard_map.76 = bf16[16,384,128]{2,1,0:T(8,128)(2,1)} custom-call(bf16[2048,128]{1,0:T(8,128)(2,1)} %bitcast.14, bf16[256,128]{1,0:T(8,128)(2,1)} %bitcast.15, bf16[256,128]{1,0:T(8,128)(2,1)} %bitcast.16), custom_call_target="tpu_custom_call" | custom-call | tf_op jit(solution)/shard_map/pallas_call | solution.py:238
  3.5 7.9 %all-to-all-start = ((bf16[16,384,128]{2,1,0:T(8,128)(2,1)}), bf16[16,384,128]{2,1,0:T(8,128)(2,1)S(1)}, u32[]{:S(2)}, u32[]{:S(2)}) async-start(bf16[16,384,128]{2,1,0:T(8,128)(2,1)} %shard_map.76), calls=%async_computation | async-start | bytes 3145728 | tf_op jit(solution)/shard_map/all_to_all | solution.py:299
  11.4 0.7 dynamic-slice_bitcast_fusion
  12.1 38.8 %all-to-all-done.x_ref = bf16[16,384,128]{2,1,0:T(8,128)(2,1)S(1)} async-done(((bf16[16,384,128]{2,1,0:T(8,128)(2,1)}), bf16[16,384,128]{2,1,0:T(8,128)(2,1)S(1)}, u32[]{:S(2)}, u32[]{:S(2)}) %all-to-all-start) | async-done | bytes 1572896 | tf_op jit(solution)/shard_map/all_to_all | solution.py:299
  51.0 7.2 %shard_map.77 = bf16[136,128]{1,0:T(8,128)(2,1)S(1)} custom-call(bf16[16,384,128]{2,1,0:T(8,128)(2,1)S(1)} %all-to-all-done.x_ref, bf16[64,128]{1,0:T(8,128)(2,1)S(1)} %get-tuple-element.10.mq_ref, bf16[64,128]{1,0:T(8,128)(2,1)S(1)} %get-tuple-element.9.mk_ref), custom_call_target="tpu_custom_call" | custom-call | tf_op jit(solution)/shard_map/pallas_call | solution.py:238
  58.2 20.8 %all_to_all.15.x_ref = bf16[8,136,128]{2,1,0:T(8,128)(2,1)S(1)} all-to-all(bf16[8,136,128]{2,1,0:T(8,128)(2,1)S(1)} %broadcast_in_dim.2), channel_id=1, replica_groups=mesh['dp'=8,'ctx'=16,'head'=4] {'dp'}, dimensions={0} | all-to-all | bytes 557056 | tf_op jit(solution)/shard_map/all_to_all | solution.py:302
  79.0 0.1 shard_map.78
  79.1 22.0 %all_to_all.16.x_ref = bf16[16,136,128]{2,1,0:T(8,128)(2,1)S(1)} all-to-all(bf16[16,136,128]{2,1,0:T(8,128)(2,1)S(1)} %shard_map.78), channel_id=1, replica_groups=mesh['dp'=8,'ctx'=16,'head'=4] {'ctx'}, dimensions={0} | all-to-all | bytes 1114112 | tf_op jit(solution)/shard_map/all_to_all | solution.py:304
  101.1 1.5 %shard_map.79 = (f32[16,64,128]{2,1,0:T(8,128)}, f32[16,64,128]{2,1,0:T(8,128)}, f32[1,16]{1,0:T(1,128)}) custom-call(bf16[16,136,128]{2,1,0:T(8,128)(2,1)S(1)} %all_to_all.16.x_ref), custom_call_target="tpu_custom_call" | custom-call | tf_op jit(solution)/shard_map/pallas_call | solution.py:238
  (1 shorter events, 0.0 us)
Async XLA Ops:
  3.5 47.5 %all-to-all-start = ((bf16[16,384,128]{2,1,0:T(8,128)(2,1)}), bf16[16,384,128]{2,1,0:T(8,128)(2,1)S(1)}, u32[]{:S(2)}, u32[]{:S(2)}) async-start(bf16[16,384,128]{2,1,0:T(8,128)(2,1)} %shard_map.76), calls=%async_computation | async-start | bytes 3145728 | tf_op jit(solution)/shard_map/all_to_all | solution.py:299

commit v4 on v3

--- a/solution.py
+++ b/solution.py
@@ -11,7 +11,8 @@
 F32 = jnp.float32
 BF16 = jnp.bfloat16
 CHUNK = 256
-LOSS_ROWS = 8
+EXCHANGE = [0, 14, 2, 12, 4, 10, 6, 8, 1, 15, 3, 13, 5, 11, 7, 9]
+GATHER = [10, 5, 0, 1, 9, 4, 6, 2, 3, 15, 11, 7, 12, 8, 13, 14]
 
 
 def nn(left, right):
@@ -76,8 +77,8 @@
     logits = nt(mapping_t, inputs)
     positive = jnp.exp(logits - jnp.max(logits, 0, keepdims=True))
     negative = jnp.exp(jnp.min(logits, 0, keepdims=True) - logits)
-    positive = positive / jnp.sum(positive, 0, keepdims=True)
-    negative = negative / jnp.sum(negative, 0, keepdims=True)
+    positive = positive * (1.0 / jnp.sum(positive, 0, keepdims=True))
+    negative = negative * (1.0 / jnp.sum(negative, 0, keepdims=True))
     return positive, negative
 
 
@@ -99,8 +100,9 @@
     scale = size**-0.5 * math.log2(math.e)
 
     def part(which, first, last):
-        piece = x_ref[first * per : last * per, which * tokens : (which + 1) * tokens, :]
-        return piece.reshape((last - first) * CHUNK, size)
+        slots = [EXCHANGE.index(block) for block in range(first * per, last * per)]
+        rows = slice(which * tokens, (which + 1) * tokens)
+        return jnp.concatenate([x_ref[slot, rows, :] for slot in slots], 0)
 
     def each(make):
         return [make(c) for c in chunks]
@@ -137,14 +139,14 @@
         target = nn(expos[-1].astype(BF16), part(2, c, c + 1))
         if c:
             target = target + nn(expos[0].astype(BF16), part(2, 0, c))
-        return target / mass
+        return target * (1.0 / mass)
 
     def score(c):
         return halves(jnp.where(causal, nn(phi_q[c], phi_kt[c]), 0.0))
 
     blocks_of = each(block)
     peaks = each(peak)
-    made, target = zip(*each(lambda c: (feature(c), teacher(c))))
+    target, made = zip(*each(lambda c: (teacher(c), feature(c))))
     k_halves, q_halves, phi_kt, phi_qt, phi_q = zip(*made)
     k_up, k_down = zip(*k_halves)
     q_up, q_down = zip(*q_halves)
@@ -179,51 +181,50 @@
     )
     query_map = sum(each(lambda c: wide_nn(logit_gradient(q_up[c], q_down[c], q_gradient[c]), q[c])))
     key_map = sum(each(lambda c: wide_nn(logit_gradient(k_up[c], k_down[c], k_gradient[c]), k[c])))
-    maps = jnp.concatenate([query_map, key_map], 0)
-    out_ref[0:size, :] = maps.astype(BF16)
     total = jnp.sum(jnp.sum(loss, 0, keepdims=True), 1, keepdims=True) * (1.0 / token_count)
-    out_ref[size:, :] = loss_rows(total)
-
-
-def loss_rows(total):
-    high = jnp.broadcast_to(total, (LOSS_ROWS, 128)).astype(BF16).astype(F32)
-    low = total - high
-    row = lax.broadcasted_iota(jnp.int32, (LOSS_ROWS, 128), 0)
-    return jnp.where(row == 0, high, jnp.where(row == 1, low, 0.0)).astype(BF16)
+    out_ref[...] = with_loss(jnp.concatenate([query_map, key_map], 0), total)
+
+
+def with_loss(maps, total):
+    last = maps.shape[0] // 2 - 1
+    high = total.astype(BF16).astype(F32)
+    row = lax.broadcasted_iota(jnp.int32, maps.shape, 0)
+    col = lax.broadcasted_iota(jnp.int32, maps.shape, 1)
+    maps = jnp.where((row == last) & (col == 0), high, maps)
+    return jnp.where((row == last) & (col == 1), total - high, maps).astype(BF16)
 
 
 def add_kernel(x_ref, out_ref):
-    size = x_ref.shape[1] - LOSS_ROWS
     total = x_ref[0].astype(F32)
     for place in range(1, x_ref.shape[0]):
         total = total + x_ref[place].astype(F32)
-    maps = total[:size].astype(BF16)
-    loss = loss_rows(total[size : size + 1, 0:1] + total[size + 1 : size + 2, 0:1])
+    last = total.shape[0] // 2 - 1
+    maps = with_loss(total, total[last : last + 1, 0:1] + total[last : last + 1, 1:2])
     for place in range(out_ref.shape[0]):
-        out_ref[place, 0:size, :] = maps
-        out_ref[place, size:, :] = loss
+        out_ref[place] = maps
 
 
 def spread_kernel(x_ref, query_hbm, key_hbm, loss_ref, query_ref, key_ref, sems):
-    heads, feat, _ = query_ref.shape
-    size = 2 * feat
-    parts = sems.shape[1]
-    each = heads // parts
+    heads, feat, size = query_ref.shape
+    row = lax.broadcasted_iota(jnp.int32, (feat, size), 0)
+    col = lax.broadcasted_iota(jnp.int32, (feat, size), 1)
+    swapped = (row == feat - 1) & (col < 2)
     lane = lax.broadcasted_iota(jnp.int32, (1, heads), 1)
     loss = jnp.zeros((1, heads), F32)
-    copies = []
-    for part in range(parts):
-        own = pl.ds(part * each, each)
-        for head in range(part * each, (part + 1) * each):
-            query_ref[head] = x_ref[head, 0:feat, :].astype(F32)
-            key_ref[head] = x_ref[head, feat:size, :].astype(F32)
-        for place, (source, target) in enumerate(((query_ref, query_hbm), (key_ref, key_hbm))):
-            copies.append(pltpu.make_async_copy(source.at[own], target.at[own], sems.at[place, part]))
-            copies[-1].start()
     for head in range(heads):
-        tail = x_ref[head, size:, :].astype(F32)
-        loss = jnp.where(lane == head, tail[0:1, :heads] + tail[1:2, :heads], loss)
+        slot = GATHER.index(EXCHANGE[head])
+        maps = x_ref[slot, 0:feat, :].astype(F32)
+        rest = jnp.sum(jnp.where(swapped, 0.0, maps), 0, keepdims=True)
+        query_ref[head] = jnp.where(swapped, -rest, maps)
+        key_ref[head] = x_ref[slot, feat:, :].astype(F32)
+        loss = jnp.where(lane == head, maps[feat - 1 :, 0:1] + maps[feat - 1 :, 1:2], loss)
     loss_ref[...] = loss
+    copies = [
+        pltpu.make_async_copy(source, target, sems.at[place])
+        for place, (source, target) in enumerate(((query_ref, query_hbm), (key_ref, key_hbm)))
+    ]
+    for copy in copies:
+        copy.start()
     for copy in copies:
         copy.wait()
 
@@ -250,7 +251,7 @@
     chunks = blocks * rows // 3 // CHUNK
     return call(
         functools.partial(head_kernel, token_count),
-        jax.ShapeDtypeStruct((size + LOSS_ROWS, size), BF16),
+        jax.ShapeDtypeStruct((size, size), BF16),
         [sequence, own_query, own_key],
         (),
         48,
@@ -280,7 +281,7 @@
         spread_kernel,
         [shape(maps, F32), shape(maps, F32), shape((1, heads), F32)],
         [gathered],
-        [pltpu.VMEM(maps, F32), pltpu.VMEM(maps, F32), pltpu.SemaphoreType.DMA((2, 2))],
+        [pltpu.VMEM(maps, F32), pltpu.VMEM(maps, F32), pltpu.SemaphoreType.DMA((2,))],
         out_specs=[HBM, HBM, VMEM],
     )
 
@@ -293,15 +294,16 @@
     token_count = dp * ctx * tokens
     shape = jax.ShapeDtypeStruct
     packed = pack_call(queries, keys, values)
-    mine = lax.axis_index("ctx")
+    places = [EXCHANGE.index(block) for block in range(ctx)]
+    mine = jnp.asarray(places, jnp.int32)[lax.axis_index("ctx")]
     own_query = lax.dynamic_index_in_dim(jnp.swapaxes(map_query, 1, 2), mine, 0, False)
     own_key = lax.dynamic_index_in_dim(jnp.swapaxes(map_key, 1, 2), mine, 0, False)
-    sequence = lax.all_to_all(packed, "ctx", 0, 0, tiled=True)
+    sequence = lax.all_to_all(packed, "ctx", 0, 0, tiled=True, axis_index_groups=[EXCHANGE])
     part = head_call(sequence, own_query, own_key, token_count)
     parts = jnp.broadcast_to(part[None], (dp,) + part.shape)
     parts = lax.all_to_all(parts, "dp", 0, 0, tiled=True)
     whole = call(add_kernel, shape((ctx,) + part.shape, BF16), [parts])
-    gathered = lax.all_to_all(whole, "ctx", 0, 0, tiled=True)
+    gathered = lax.all_to_all(whole, "ctx", 0, 0, tiled=True, axis_index_groups=[GATHER])
     grad_query, grad_key, loss = spread_call(gathered, feat)
     return jnp.swapaxes(grad_query, 1, 2), jnp.swapaxes(grad_key, 1, 2), loss.reshape(heads)
 

time: 103 us -> 96.5 us (0.937)
  blocking collectives: 42.8 us -> 37 us
  waiting for transfers between devices: 38.8 us -> 35.7 us
  between operations: 0.67 us -> 2.63 us
    all_to_all x1, blocking collectives: 22 us -> 16.4 us  [shards(): lax.all_to_all(whole, 'ctx', 0, 0, tiled=True, axis_index_groups=[GATHER])]
    all_to_all x1, waiting for transfers between devices: 38.8 us -> 35.7 us  [shards(): lax.all_to_all(packed, 'ctx', 0, 0, tiled=True, axis_index_groups=[EXCHAN...]
where the time goes in v4:
time: 96.5 us; the launch traced here: 96.1 us
  blocking collectives  37 us (38%)
  waiting for transfers between devices  35.7 us (37%)
  Pallas kernels  11.6 us (12%)
  starting transfers between devices  7.85 us (8%)
  between operations  2.63 us (3%)
  local copies, waits for them, and re-layouts  1.37 us (1%)
    all_to_all x1, waiting for transfers between devices, shards(): lax.all_to_all(packed, 'ctx', 0, 0, tiled=True, axis_index_groups=[EXCHAN...  35.7 us
    all_to_all x1, blocking collectives, shards(): parts = lax.all_to_all(parts, 'dp', 0, 0, tiled=True)  20.6 us
    all_to_all x1, blocking collectives, shards(): lax.all_to_all(whole, 'ctx', 0, 0, tiled=True, axis_index_groups=[GATHER])  16.4 us
    pallas_call x4, Pallas kernels, call(): pl.pallas_call(kernel, out_shape=shapes, in_specs=in_specs or [VMEM] * le...  11.6 us
    all_to_all x1, starting transfers between devices, shards(): lax.all_to_all(packed, 'ctx', 0, 0, tiled=True, axis_index_groups=[EXCHAN...  7.85 us
  transfers between devices with their start and end apart: 1, of which 1 were waited for; matrix products, arithmetic and copies ran while one was open for 1% of the time, Pallas kernels for 0%

profile of v4, /device:TPU:4, one launch (start us, length us, event | category | flops | bytes accessed | tf_op | source)
XLA Modules:
  0.0 96.1 jit_solution(5199952330894127930)
XLA Ops:
  0.6 2.9 %shard_map.85 = bf16[16,384,128]{2,1,0:T(8,128)(2,1)} custom-call(bf16[2048,128]{1,0:T(8,128)(2,1)} %bitcast.15, bf16[256,128]{1,0:T(8,128)(2,1)} %bitcast.16, bf16[256,128]{1,0:T(8,128)(2,1)} %bitcast.17), custom_call_target="tpu_custom_call" | custom-call | tf_op jit(solution)/shard_map/pallas_call | solution.py:239
  3.5 0.0 copy-start
  3.5 7.9 %all-to-all-start = ((bf16[16,384,128]{2,1,0:T(8,128)(2,1)}), bf16[16,384,128]{2,1,0:T(8,128)(2,1)S(1)}, u32[]{:S(2)}, u32[]{:S(2)}) async-start(bf16[16,384,128]{2,1,0:T(8,128)(2,1)} %shard_map.85), calls=%async_computation | async-start | bytes 3145728 | tf_op jit(solution)/shard_map/all_to_all | solution.py:301
  11.4 0.0 copy-done
  11.4 0.6 dynamic_slice.10
  13.9 0.7 dynamic-slice_bitcast_fusion
  14.7 35.7 %all-to-all-done.x_ref = bf16[16,384,128]{2,1,0:T(8,128)(2,1)S(1)} async-done(((bf16[16,384,128]{2,1,0:T(8,128)(2,1)}), bf16[16,384,128]{2,1,0:T(8,128)(2,1)S(1)}, u32[]{:S(2)}, u32[]{:S(2)}) %all-to-all-start) | async-done | bytes 1572896 | tf_op jit(solution)/shard_map/all_to_all | solution.py:301
  50.3 7.0 %shard_map.86 = bf16[128,128]{1,0:T(8,128)(2,1)S(1)} custom-call(bf16[16,384,128]{2,1,0:T(8,128)(2,1)S(1)} %all-to-all-done.x_ref, bf16[64,128]{1,0:T(8,128)(2,1)S(1)} %get-tuple-element.10.mq_ref, bf16[64,128]{1,0:T(8,128)(2,1)S(1)} %get-tuple-element.9.mk_ref), custom_call_target="tpu_custom_call" | custom-call | tf_op jit(solution)/shard_map/pallas_call | solution.py:239
  57.4 20.6 %all_to_all.15.x_ref = bf16[8,128,128]{2,1,0:T(8,128)(2,1)S(1)} all-to-all(bf16[8,128,128]{2,1,0:T(8,128)(2,1)S(1)} %broadcast_in_dim.2), channel_id=1, replica_groups=mesh['dp'=8,'ctx'=16,'head'=4] {'dp'}, dimensions={0} | all-to-all | bytes 524288 | tf_op jit(solution)/shard_map/all_to_all | solution.py:304
  78.0 0.1 shard_map.87
  78.1 16.4 %all_to_all.16.x_ref = bf16[16,128,128]{2,1,0:T(8,128)(2,1)S(1)} all-to-all(bf16[16,128,128]{2,1,0:T(8,128)(2,1)S(1)} %shard_map.87), channel_id=1, replica_groups={{40,20,0,4,36,16,24,8,12,60,44,28,48,32,52,56},{41,21,1,5,37,17,25,9,13..., dimensions={0} | all-to-all | bytes 1048576 | tf_op jit(solution)/shard_map/all_to_all | solution.py:306
  94.6 1.6 %shard_map.88 = (f32[16,64,128]{2,1,0:T(8,128)}, f32[16,64,128]{2,1,0:T(8,128)}, f32[1,16]{1,0:T(1,128)}) custom-call(bf16[16,128,128]{2,1,0:T(8,128)(2,1)S(1)} %all_to_all.16.x_ref), custom_call_target="tpu_custom_call" | custom-call | tf_op jit(solution)/shard_map/pallas_call | solution.py:239
  (1 shorter events, 0.0 us)
Async XLA Ops:
  3.5 7.9 %copy-start = (s32[16]{0:T(128)S(1)}, s32[16]{0:T(128)}, u32[]{:S(2)}) copy-start(s32[16]{0:T(128)} %constant.18.clone) | copy-start | bytes 196
  3.5 46.8 %all-to-all-start = ((bf16[16,384,128]{2,1,0:T(8,128)(2,1)}), bf16[16,384,128]{2,1,0:T(8,128)(2,1)S(1)}, u32[]{:S(2)}, u32[]{:S(2)}) async-start(bf16[16,384,128]{2,1,0:T(8,128)(2,1)} %shard_map.85), calls=%async_computation | async-start | bytes 3145728 | tf_op jit(solution)/shard_map/all_to_all | solution.py:301

commit v5 on v4

--- a/solution.py
+++ b/solution.py
@@ -11,8 +11,9 @@
 F32 = jnp.float32
 BF16 = jnp.bfloat16
 CHUNK = 256
-EXCHANGE = [0, 14, 2, 12, 4, 10, 6, 8, 1, 15, 3, 13, 5, 11, 7, 9]
-GATHER = [10, 5, 0, 1, 9, 4, 6, 2, 3, 15, 11, 7, 12, 8, 13, 14]
+EXCHANGE = [8, 6, 10, 4, 12, 2, 14, 0, 9, 7, 11, 5, 13, 3, 15, 1]
+GATHER = [8, 6, 10, 4, 12, 2, 14, 0, 9, 7, 11, 5, 13, 3, 15, 1]
+ADD = [6, 3, 0, 5, 7, 1, 4, 2]
 
 
 def nn(left, right):
@@ -301,7 +302,7 @@
     sequence = lax.all_to_all(packed, "ctx", 0, 0, tiled=True, axis_index_groups=[EXCHANGE])
     part = head_call(sequence, own_query, own_key, token_count)
     parts = jnp.broadcast_to(part[None], (dp,) + part.shape)
-    parts = lax.all_to_all(parts, "dp", 0, 0, tiled=True)
+    parts = lax.all_to_all(parts, "dp", 0, 0, tiled=True, axis_index_groups=[ADD])
     whole = call(add_kernel, shape((ctx,) + part.shape, BF16), [parts])
     gathered = lax.all_to_all(whole, "ctx", 0, 0, tiled=True, axis_index_groups=[GATHER])
     grad_query, grad_key, loss = spread_call(gathered, feat)

time: 96.5 us -> 93.1 us (0.965)
  waiting for transfers between devices: 35.7 us -> 31.6 us
  starting transfers between devices: 7.85 us -> 9.37 us
    all_to_all x1, waiting for transfers between devices: 35.7 us -> 31.6 us  [shards(): lax.all_to_all(packed, 'ctx', 0, 0, tiled=True, axis_index_groups=[EXCHAN...]
    all_to_all x1, blocking collectives: 20.6 us -> 18.1 us  [shards(): lax.all_to_all(parts, 'dp', 0, 0, tiled=True, axis_index_groups=[ADD])]
    all_to_all x1, blocking collectives: 16.4 us -> 18 us  [shards(): lax.all_to_all(whole, 'ctx', 0, 0, tiled=True, axis_index_groups=[GATHER])]
    all_to_all x1, starting transfers between devices: 7.85 us -> 9.37 us  [shards(): lax.all_to_all(packed, 'ctx', 0, 0, tiled=True, axis_index_groups=[EXCHAN...]
where the time goes in v5:
time: 93.1 us; the launch traced here: 92.6 us
  blocking collectives  36.1 us (39%)
  waiting for transfers between devices  31.6 us (34%)
  Pallas kernels  11.6 us (12%)
  starting transfers between devices  9.37 us (10%)
  between operations  2.62 us (3%)
  local copies, waits for them, and re-layouts  1.37 us (1%)
    all_to_all x1, waiting for transfers between devices, shards(): lax.all_to_all(packed, 'ctx', 0, 0, tiled=True, axis_index_groups=[EXCHAN...  31.6 us
    all_to_all x1, blocking collectives, shards(): lax.all_to_all(parts, 'dp', 0, 0, tiled=True, axis_index_groups=[ADD])  18.1 us
    all_to_all x1, blocking collectives, shards(): lax.all_to_all(whole, 'ctx', 0, 0, tiled=True, axis_index_groups=[GATHER])  18 us
    pallas_call x4, Pallas kernels, call(): pl.pallas_call(kernel, out_shape=shapes, in_specs=in_specs or [VMEM] * le...  11.6 us
    all_to_all x1, starting transfers between devices, shards(): lax.all_to_all(packed, 'ctx', 0, 0, tiled=True, axis_index_groups=[EXCHAN...  9.37 us
  transfers between devices with their start and end apart: 1, of which 1 were waited for; matrix products, arithmetic and copies ran while one was open for 1% of the time, Pallas kernels for 0%

profile of v5, /device:TPU:4, one launch (start us, length us, event | category | flops | bytes accessed | tf_op | source)
XLA Modules:
  0.0 92.6 jit_solution(1148056610307312856)
XLA Ops:
  0.6 2.9 %shard_map.85 = bf16[16,384,128]{2,1,0:T(8,128)(2,1)} custom-call(bf16[2048,128]{1,0:T(8,128)(2,1)} %bitcast.15, bf16[256,128]{1,0:T(8,128)(2,1)} %bitcast.16, bf16[256,128]{1,0:T(8,128)(2,1)} %bitcast.17), custom_call_target="tpu_custom_call" | custom-call | tf_op jit(solution)/shard_map/pallas_call | solution.py:240
  3.5 0.0 copy-start
  3.5 9.4 %all-to-all-start = ((bf16[16,384,128]{2,1,0:T(8,128)(2,1)}), bf16[16,384,128]{2,1,0:T(8,128)(2,1)S(1)}, u32[]{:S(2)}, u32[]{:S(2)}) async-start(bf16[16,384,128]{2,1,0:T(8,128)(2,1)} %shard_map.85), calls=%async_computation | async-start | bytes 3145728 | tf_op jit(solution)/shard_map/all_to_all | solution.py:302
  12.9 0.0 copy-done
  12.9 0.6 dynamic_slice.10
  15.4 0.7 dynamic-slice_bitcast_fusion
  16.2 31.6 %all-to-all-done.x_ref = bf16[16,384,128]{2,1,0:T(8,128)(2,1)S(1)} async-done(((bf16[16,384,128]{2,1,0:T(8,128)(2,1)}), bf16[16,384,128]{2,1,0:T(8,128)(2,1)S(1)}, u32[]{:S(2)}, u32[]{:S(2)}) %all-to-all-start) | async-done | bytes 1572896 | tf_op jit(solution)/shard_map/all_to_all | solution.py:302
  47.7 7.0 %shard_map.86 = bf16[128,128]{1,0:T(8,128)(2,1)S(1)} custom-call(bf16[16,384,128]{2,1,0:T(8,128)(2,1)S(1)} %all-to-all-done.x_ref, bf16[64,128]{1,0:T(8,128)(2,1)S(1)} %get-tuple-element.10.mq_ref, bf16[64,128]{1,0:T(8,128)(2,1)S(1)} %get-tuple-element.9.mk_ref), custom_call_target="tpu_custom_call" | custom-call | tf_op jit(solution)/shard_map/pallas_call | solution.py:240
  54.8 18.1 %all_to_all.15.x_ref = bf16[8,128,128]{2,1,0:T(8,128)(2,1)S(1)} all-to-all(bf16[8,128,128]{2,1,0:T(8,128)(2,1)S(1)} %broadcast_in_dim.2), channel_id=1, replica_groups={{384,192,0,320,448,64,256,128},{385,193,1,321,449,65,257,129},{386,194,..., dimensions={0} | all-to-all | bytes 524288 | tf_op jit(solution)/shard_map/all_to_all | solution.py:305
  72.9 0.1 shard_map.87
  73.0 18.0 %all_to_all.16.x_ref = bf16[16,128,128]{2,1,0:T(8,128)(2,1)S(1)} all-to-all(bf16[16,128,128]{2,1,0:T(8,128)(2,1)S(1)} %shard_map.87), channel_id=1, replica_groups={{32,24,40,16,48,8,56,0,36,28,44,20,52,12,60,4},{33,25,41,17,49,9,57,1,3..., dimensions={0} | all-to-all | bytes 1048576 | tf_op jit(solution)/shard_map/all_to_all | solution.py:307
  91.1 1.6 %shard_map.88 = (f32[16,64,128]{2,1,0:T(8,128)}, f32[16,64,128]{2,1,0:T(8,128)}, f32[1,16]{1,0:T(1,128)}) custom-call(bf16[16,128,128]{2,1,0:T(8,128)(2,1)S(1)} %all_to_all.16.x_ref), custom_call_target="tpu_custom_call" | custom-call | tf_op jit(solution)/shard_map/pallas_call | solution.py:240
  (1 shorter events, 0.0 us)
Async XLA Ops:
  3.5 9.4 %copy-start = (s32[16]{0:T(128)S(1)}, s32[16]{0:T(128)}, u32[]{:S(2)}) copy-start(s32[16]{0:T(128)} %constant.18.clone) | copy-start | bytes 196
  3.5 44.2 %all-to-all-start = ((bf16[16,384,128]{2,1,0:T(8,128)(2,1)}), bf16[16,384,128]{2,1,0:T(8,128)(2,1)S(1)}, u32[]{:S(2)}, u32[]{:S(2)}) async-start(bf16[16,384,128]{2,1,0:T(8,128)(2,1)} %shard_map.85), calls=%async_computation | async-start | bytes 3145728 | tf_op jit(solution)/shard_map/all_to_all | solution.py:302

commit v6 on v5

--- a/solution.py
+++ b/solution.py
@@ -13,7 +13,7 @@
 CHUNK = 256
 EXCHANGE = [8, 6, 10, 4, 12, 2, 14, 0, 9, 7, 11, 5, 13, 3, 15, 1]
 GATHER = [8, 6, 10, 4, 12, 2, 14, 0, 9, 7, 11, 5, 13, 3, 15, 1]
-ADD = [6, 3, 0, 5, 7, 1, 4, 2]
+ADD = [6, 1, 4, 7, 5, 3, 0, 2]
 
 
 def nn(left, right):

time: 93.1 us -> 93.1 us (level)
  no operation moved by 1% of the time
where the time goes in v6:
time: 93.1 us; the launch traced here: 92.6 us
  blocking collectives  36.1 us (39%)
  waiting for transfers between devices  31.6 us (34%)
  Pallas kernels  11.6 us (12%)
  starting transfers between devices  9.37 us (10%)
  between operations  2.62 us (3%)
  local copies, waits for them, and re-layouts  1.37 us (1%)
    all_to_all x1, waiting for transfers between devices, shards(): lax.all_to_all(packed, 'ctx', 0, 0, tiled=True, axis_index_groups=[EXCHAN...  31.6 us
    all_to_all x1, blocking collectives, shards(): lax.all_to_all(parts, 'dp', 0, 0, tiled=True, axis_index_groups=[ADD])  18.7 us
    all_to_all x1, blocking collectives, shards(): lax.all_to_all(whole, 'ctx', 0, 0, tiled=True, axis_index_groups=[GATHER])  17.5 us
    pallas_call x4, Pallas kernels, call(): pl.pallas_call(kernel, out_shape=shapes, in_specs=in_specs or [VMEM] * le...  11.6 us
    all_to_all x1, starting transfers between devices, shards(): lax.all_to_all(packed, 'ctx', 0, 0, tiled=True, axis_index_groups=[EXCHAN...  9.37 us
  transfers between devices with their start and end apart: 1, of which 1 were waited for; matrix products, arithmetic and copies ran while one was open for 1% of the time, Pallas kernels for 0%

profile of v6, /device:TPU:4, one launch (start us, length us, event | category | flops | bytes accessed | tf_op | source)
XLA Modules:
  0.0 92.6 jit_solution(9881367045162931776)
XLA Ops:
  0.6 2.9 %shard_map.85 = bf16[16,384,128]{2,1,0:T(8,128)(2,1)} custom-call(bf16[2048,128]{1,0:T(8,128)(2,1)} %bitcast.15, bf16[256,128]{1,0:T(8,128)(2,1)} %bitcast.16, bf16[256,128]{1,0:T(8,128)(2,1)} %bitcast.17), custom_call_target="tpu_custom_call" | custom-call | tf_op jit(solution)/shard_map/pallas_call | solution.py:240
  3.5 0.0 copy-start
  3.5 9.4 %all-to-all-start = ((bf16[16,384,128]{2,1,0:T(8,128)(2,1)}), bf16[16,384,128]{2,1,0:T(8,128)(2,1)S(1)}, u32[]{:S(2)}, u32[]{:S(2)}) async-start(bf16[16,384,128]{2,1,0:T(8,128)(2,1)} %shard_map.85), calls=%async_computation | async-start | bytes 3145728 | tf_op jit(solution)/shard_map/all_to_all | solution.py:302
  12.9 0.0 copy-done
  12.9 0.6 dynamic_slice.10
  15.4 0.7 dynamic-slice_bitcast_fusion
  16.2 31.6 %all-to-all-done.x_ref = bf16[16,384,128]{2,1,0:T(8,128)(2,1)S(1)} async-done(((bf16[16,384,128]{2,1,0:T(8,128)(2,1)}), bf16[16,384,128]{2,1,0:T(8,128)(2,1)S(1)}, u32[]{:S(2)}, u32[]{:S(2)}) %all-to-all-start) | async-done | bytes 1572896 | tf_op jit(solution)/shard_map/all_to_all | solution.py:302
  47.7 7.0 %shard_map.86 = bf16[128,128]{1,0:T(8,128)(2,1)S(1)} custom-call(bf16[16,384,128]{2,1,0:T(8,128)(2,1)S(1)} %all-to-all-done.x_ref, bf16[64,128]{1,0:T(8,128)(2,1)S(1)} %get-tuple-element.10.mq_ref, bf16[64,128]{1,0:T(8,128)(2,1)S(1)} %get-tuple-element.9.mk_ref), custom_call_target="tpu_custom_call" | custom-call | tf_op jit(solution)/shard_map/pallas_call | solution.py:240
  54.8 18.7 %all_to_all.15.x_ref = bf16[8,128,128]{2,1,0:T(8,128)(2,1)S(1)} all-to-all(bf16[8,128,128]{2,1,0:T(8,128)(2,1)S(1)} %broadcast_in_dim.2), channel_id=1, replica_groups={{384,64,256,448,320,192,0,128},{385,65,257,449,321,193,1,129},{386,66,2..., dimensions={0} | all-to-all | bytes 524288 | tf_op jit(solution)/shard_map/all_to_all | solution.py:305
  73.5 0.1 shard_map.87
  73.6 17.5 %all_to_all.16.x_ref = bf16[16,128,128]{2,1,0:T(8,128)(2,1)S(1)} all-to-all(bf16[16,128,128]{2,1,0:T(8,128)(2,1)S(1)} %shard_map.87), channel_id=1, replica_groups={{32,24,40,16,48,8,56,0,36,28,44,20,52,12,60,4},{33,25,41,17,49,9,57,1,3..., dimensions={0} | all-to-all | bytes 1048576 | tf_op jit(solution)/shard_map/all_to_all | solution.py:307
  91.1 1.6 %shard_map.88 = (f32[16,64,128]{2,1,0:T(8,128)}, f32[16,64,128]{2,1,0:T(8,128)}, f32[1,16]{1,0:T(1,128)}) custom-call(bf16[16,128,128]{2,1,0:T(8,128)(2,1)S(1)} %all_to_all.16.x_ref), custom_call_target="tpu_custom_call" | custom-call | tf_op jit(solution)/shard_map/pallas_call | solution.py:240
  (1 shorter events, 0.0 us)
Async XLA Ops:
  3.5 9.4 %copy-start = (s32[16]{0:T(128)S(1)}, s32[16]{0:T(128)}, u32[]{:S(2)}) copy-start(s32[16]{0:T(128)} %constant.18.clone) | copy-start | bytes 196
  3.5 44.2 %all-to-all-start = ((bf16[16,384,128]{2,1,0:T(8,128)(2,1)}), bf16[16,384,128]{2,1,0:T(8,128)(2,1)S(1)}, u32[]{:S(2)}, u32[]{:S(2)}) async-start(bf16[16,384,128]{2,1,0:T(8,128)(2,1)} %shard_map.85), calls=%async_computation | async-start | bytes 3145728 | tf_op jit(solution)/shard_map/all_to_all | solution.py:302
